TPU v7x, 32 devices: a whole 2x2x4 slice. The times are simulated.
32 devices in a mesh: row: 4 (over y, core), col: 8 (over z, x).
Axes of the slice: x: 2, y: 2, z: 4, core: 2. Of those that a mesh axis runs over, the one named last changes fastest.
Arguments:
- object_field: float32 [2, 1024, 2048], P(None, 'row', 'col'), may hold values from -4.2 to 4.2
- probe_modes: float32 [2, 8, 256, 256], replicated, may hold values from -1.5 to 1.5
- patterns: float32 [64, 256, 256], P(('row', 'col')), may hold values from 0.3 to 3
- offsets: int32 [2, 64], P(None, ('row', 'col')), may hold values from 0 to 1792, as said below
- counts: int32 [32], P(('row', 'col')), may hold values from 1 to 2, as said below
Outputs:
- new_object: float32 [2, 1024, 2048], P(None, 'row', 'col')
- new_probe: float32 [2, 8, 256, 256], replicated
Inputs may be any that keep to these rules, and one draw needn't show every extreme that they name: `offsets`: A slot of the device of tile row r and tile column c has row offset in [r * 256, (r + 1) * 256) and column offset in [c * 256, (c + 1) * 256); every patch lies inside the object. `counts`: A device's live slots are its first ones.
All inputs are finite; a program needn't handle non-finite values.
Results may differ from a plain program's by a relative error of at most 0.0001.
Values sent between devices are 32-bit elements; how exact they have to be, the bound alone decides.
A program may use at most 128 MiB of HBM per device.

v0:
```python
import math

import jax
import jax.numpy as jnp
from jax import lax
from jax.sharding import PartitionSpec as P

INTENSITY_FLOOR = 0.1
OBJECT_DELTA = 0.5
PROBE_DELTA = 1.0
SMOOTH_WEIGHT = 0.1
HIGHEST = lax.Precision.HIGHEST


def shifted(value, axis, steps):
    count = lax.axis_size(axis)
    first, last = (max(0, -steps), min(count, count - steps))
    return lax.ppermute(value, axis, [(source, source + steps) for source in range(first, last)])


def extended_2(value, sides, width):
    for axis, dim in sides:
        size, length = (lax.axis_size(axis), value.shape[dim])
        up = [(i, (i + 1) % size) for i in range(size - 1)]
        down = [(j, i) for i, j in up]
        last = lax.slice_in_dim(value, length - width, length, axis=dim)
        first = lax.slice_in_dim(value, 0, width, axis=dim)
        before = lax.ppermute(last, axis, up)
        after = lax.ppermute(first, axis, down)
        value = jnp.concatenate([before, value, after], axis=dim)
    return value


def dft_tables(length):
    indices = lax.iota(jnp.int32, length)
    product = indices[:, None] * indices[None, :] % length
    angles = product.astype(jnp.float32) * (2.0 * math.pi / length)
    scaled = 1.0 / math.sqrt(length)
    return (jnp.cos(angles) * scaled, -jnp.sin(angles) * scaled)


def transform(field_real, field_imag, table_real, table_imag):
    left_real = jnp.einsum("uy,myx->mux", table_real, field_real, precision=HIGHEST) - jnp.einsum(
        "uy,myx->mux", table_imag, field_imag, precision=HIGHEST
    )
    left_imag = jnp.einsum("uy,myx->mux", table_real, field_imag, precision=HIGHEST) + jnp.einsum(
        "uy,myx->mux", table_imag, field_real, precision=HIGHEST
    )
    out_real = jnp.einsum("muy,yv->muv", left_real, table_real, precision=HIGHEST) - jnp.einsum(
        "muy,yv->muv", left_imag, table_imag, precision=HIGHEST
    )
    out_imag = jnp.einsum("muy,yv->muv", left_real, table_imag, precision=HIGHEST) + jnp.einsum(
        "muy,yv->muv", left_imag, table_real, precision=HIGHEST
    )
    return (out_real, out_imag)


def per_device(object_field, probe_modes, patterns, offsets, counts):
    tile_cells = object_field.shape[1]
    frame_cells = probe_modes.shape[-1]
    mode_count = probe_modes.shape[1]
    slot_count = patterns.shape[0]
    row_base = lax.axis_index("row") * tile_cells
    col_base = lax.axis_index("col") * tile_cells
    right_edge = shifted(object_field, "col", -1)
    widened = jnp.concatenate([object_field, right_edge], axis=2)
    lower_edge = shifted(widened, "row", -1)
    extended = jnp.concatenate([widened, lower_edge], axis=1)
    table_real, table_imag = dft_tables(frame_cells)
    probe_real = probe_modes[0]
    probe_imag = probe_modes[1]
    probe_power = jnp.sum(probe_real * probe_real + probe_imag * probe_imag, axis=0)
    live_count = counts[0]
    zero_index = jnp.int32(0)

    def update_slot(slot_index, running):
        totals, grad_real, grad_imag, object_power = running
        row_start = offsets[0, slot_index] - row_base
        col_start = offsets[1, slot_index] - col_base
        live_flag = (slot_index < live_count).astype(jnp.float32)
        object_patch = lax.dynamic_slice(
            extended, (zero_index, row_start, col_start), (2, frame_cells, frame_cells)
        )
        patch_real = object_patch[0]
        patch_imag = object_patch[1]
        wave_real = probe_real * patch_real[None] - probe_imag * patch_imag[None]
        wave_imag = probe_real * patch_imag[None] + probe_imag * patch_real[None]
        spec_real, spec_imag = transform(wave_real, wave_imag, table_real, table_imag)
        intensity = jnp.sum(spec_real * spec_real + spec_imag * spec_imag, axis=0)
        scale_ratio = patterns[slot_index] / jnp.sqrt(jnp.maximum(intensity, INTENSITY_FLOOR))
        new_real, new_imag = transform(
            spec_real * scale_ratio[None], spec_imag * scale_ratio[None], table_real, -table_imag
        )
        diff_real = (new_real - wave_real) * live_flag
        diff_imag = (new_imag - wave_imag) * live_flag
        numer_real = jnp.sum(probe_real * diff_real + probe_imag * diff_imag, axis=0)
        numer_imag = jnp.sum(probe_real * diff_imag - probe_imag * diff_real, axis=0)
        addition = jnp.stack([numer_real, numer_imag, live_flag * probe_power])
        current = lax.dynamic_slice(
            totals, (zero_index, row_start, col_start), (3, frame_cells, frame_cells)
        )
        totals = lax.dynamic_update_slice(
            totals, current + addition, (zero_index, row_start, col_start)
        )
        grad_real = grad_real + patch_real[None] * diff_real + patch_imag[None] * diff_imag
        grad_imag = grad_imag + patch_real[None] * diff_imag - patch_imag[None] * diff_real
        object_power = object_power + live_flag * (
            patch_real * patch_real + patch_imag * patch_imag
        )
        return (totals, grad_real, grad_imag, object_power)

    initial = (
        jnp.zeros((3, tile_cells + frame_cells, tile_cells + frame_cells), jnp.float32),
        jnp.zeros((mode_count, frame_cells, frame_cells), jnp.float32),
        jnp.zeros((mode_count, frame_cells, frame_cells), jnp.float32),
        jnp.zeros((frame_cells, frame_cells), jnp.float32),
    )
    totals, grad_real, grad_imag, object_power = lax.fori_loop(0, slot_count, update_slot, initial)
    arrived_rows = shifted(totals[:, tile_cells:, :], "row", 1)
    upper_part = totals[:, :tile_cells, :].at[:, :frame_cells, :].add(arrived_rows)
    arrived_cols = shifted(upper_part[:, :, tile_cells:], "col", 1)
    own_sums = upper_part[:, :, :tile_cells].at[:, :, :frame_cells].add(arrived_cols)
    denominator = own_sums[2] + OBJECT_DELTA
    updated = jnp.stack(
        [object_field[0] + own_sums[0] / denominator, object_field[1] + own_sums[1] / denominator]
    )
    padded = extended_2(updated, (("row", 1), ("col", 2)), 1)
    neighbours = (
        padded[:, 2:, 1:-1] + padded[:, :-2, 1:-1] + padded[:, 1:-1, 2:] + padded[:, 1:-1, :-2]
    )
    new_object = updated + SMOOTH_WEIGHT * (neighbours - 4.0 * updated)
    gradient = jnp.stack([grad_real, grad_imag])
    gradient_all, power_all = lax.psum((gradient, object_power), ("row", "col"))
    new_probe = probe_modes + gradient_all / (power_all[None, None] + PROBE_DELTA)
    return (new_object, new_probe)


def solution(mesh):
    return jax.shard_map(
        per_device,
        mesh=mesh,
        in_specs=(
            P(None, "row", "col"),
            P(),
            P(("row", "col"), None, None),
            P(None, ("row", "col")),
            P(("row", "col")),
        ),
        out_specs=(P(None, "row", "col"), P()),
        check_vma=False,
    )
```

profile of v0, /device:TPU:13, one launch (start us, length us, event | category | flops | bytes accessed | tf_op | source)
XLA Modules:
  0.0 420.1 jit_solution(12324615370236871564)
XLA Ops:
  7.2 3.0 collective-permute-start
  12.2 9.9 %collective-permute-done = f32[2,256,256]{2,1,0:T(8,128)S(1)} collective-permute-done((f32[2,256,256]{2,1,0:T(8,128)}, f32[2,256,256]{2,1,0:T(8,128)S(1)}, u32[]{:S(2)}, u32[]{:S(2)}) %collective-permute-start) | collective-permute-done | bytes 524320 | tf_op jit(solution)/shard_map/ppermute | solution.py:18
  23.0 4.4 %collective-permute-start.1 = (f32[2,256,512]{2,1,0:T(8,128)}, f32[2,256,512]{2,1,0:T(8,128)}, u32[]{:S(2)}, u32[]{:S(2)}) collective-permute-start(f32[2,256,512]{2,1,0:T(8,128)} %constant_dynamic-update-slice_fusion), channel_id=1, source_target_pairs={{8,0},{16,8},{24,16},{9,1},{17,9},{25,17},{10,2},{18,10},{26,18},{... | collective-permute-start | bytes 3145736 | tf_op jit(solution)/shard_map/ppermute | solution.py:18
  32.7 3.0 pad_maximum_fusion.1
  37.8 193.5 %while.26 = (s32[]{:T(128)}, f32[3,512,512]{2,1,0:T(8,128)}, f32[8,256,256]{2,1,0:T(8,128)}, f32[8,256,256]{2,1,0:T(8,128)}, f32[256,256]{1,0:T(8,128)S(1)}, /*i...) while((s32[]{:T(128)}, f32[3,512,512]{2,1,0:T(8,128)}, ...), condition=%wide.region_5.6_spmd.clone.clone, body=%wide.region_1.5_spmd.clone.clone.sunk | while | flops 25810370560 | bytes 162791936 | solution.py:118
  43.8 4.5 %fusion.247 = f32[8,256,256]{2,1,0:T(8,128)S(1)} fusion(f32[8,256,256]{2,1,0:T(8,128)S(1)} %get-tuple-element.677), kind=kOutput, calls=%fused_computation.75.clone.1 | convolution fusion | flops 1611595776 | bytes 4194304 | tf_op jit(solution)/shard_map/while/body/eval_jaxpr/uy,myx->mux/dot_general | solution.py:43
  48.3 4.4 %convolution_subtract_fusion.2 = f32[8,256,256]{2,1,0:T(8,128)S(1)} fusion(f32[8,256,256]{2,1,0:T(8,128)S(1)} %fusion.247, f32[8,256,256]{2,1,0:T(8,128)S(1)} %get-tuple-element.676), kind=kOutput, calls=%fused_computation.43.clone.1 | convolution fusion | flops 1612185600 | bytes 6291456 | tf_op jit(solution)/shard_map/while/body/eval_jaxpr/uy,myx->mux/dot_general | solution.py:43
  52.8 4.8 %fusion.245 = f32[8,256,256]{2,1,0:T(8,128)S(1)} fusion(f32[8,256,256]{2,1,0:T(8,128)S(1)} %get-tuple-element.676), kind=kOutput, calls=%fused_computation.72.clone.1 | convolution fusion | flops 1611595776 | bytes 4194304 | tf_op jit(solution)/shard_map/while/body/eval_jaxpr/uy,myx->mux/dot_general | solution.py:46
  57.6 4.5 %convolution_add_fusion.2 = f32[8,256,256]{2,1,0:T(8,128)S(1)} fusion(f32[8,256,256]{2,1,0:T(8,128)S(1)} %fusion.245, f32[8,256,256]{2,1,0:T(8,128)S(1)} %get-tuple-element.677), kind=kOutput, calls=%fused_computation.42.clone.1 | convolution fusion | flops 1612185600 | bytes 6291456 | tf_op jit(solution)/shard_map/while/body/eval_jaxpr/uy,myx->mux/dot_general | solution.py:46
  62.1 4.4 %fusion.246 = f32[8,256,256]{2,1,0:T(8,128)S(1)} fusion(f32[8,256,256]{2,1,0:T(8,128)S(1)} %convolution_add_fusion.2), kind=kOutput, calls=%fused_computation.13.clone.1 | convolution fusion | flops 1611661312 | bytes 4194304 | tf_op jit(solution)/shard_map/while/body/eval_jaxpr/muy,yv->muv/dot_general | solution.py:49
  66.5 4.7 %fusion.248 = f32[8,256,256]{2,1,0:T(8,128)S(1)} fusion(f32[8,256,256]{2,1,0:T(8,128)S(1)} %fusion.246, f32[8,256,256]{2,1,0:T(8,128)S(1)} %convolution_subtract_fusion.2), kind=kOutput, calls=%fused_computation.40.clone.1 | convolution fusion | flops 1612120064 | bytes 6291456 | tf_op jit(solution)/shard_map/while/body/eval_jaxpr/muy,yv->muv/dot_general | solution.py:49
  71.2 4.4 %fusion.249 = f32[8,256,256]{2,1,0:T(8,128)S(1)} fusion(f32[8,256,256]{2,1,0:T(8,128)S(1)} %convolution_add_fusion.2), kind=kOutput, calls=%fused_computation.11.clone.1 | convolution fusion | flops 1611595776 | bytes 4194304 | tf_op jit(solution)/shard_map/while/body/eval_jaxpr/muy,yv->muv/dot_general | solution.py:52
  75.6 4.7 %add_reduce_fusion.4 = (f32[256,256]{1,0:T(8,128)S(1)}, f32[8,256,256]{2,1,0:T(8,128)S(1)}) fusion(f32[8,256,256]{2,1,0:T(8,128)S(1)} %fusion.248, f32[8,256,256]{2,1,0:T(8,128)S(1)} %fusion.249, f32[8,256,256]{2,1,0:T(8,128)S(1)} %convolution_subtract_fusion.2), kind=kOutput, calls=%fused_computation.27.clone.1 | convolution fusion | flops 1614217216 | bytes 8650752 | tf_op jit(solution)/shard_map/while/body/eval_jaxpr/muy,yv->muv/dot_general | solution.py:52
  81.6 4.5 %fusion.254 = f32[8,256,256]{2,1,0:T(8,128)S(1)} fusion(f32[8,256,256]{2,1,0:T(8,128)S(1)} %get-tuple-element.678, f32[256,256]{1,0:T(8,128)S(1)} %fusion.250), kind=kOutput, calls=%fused_computation.32.clone.1 | convolution fusion | flops 1612251136 | bytes 4456448 | tf_op jit(solution)/shard_map/while/body/eval_jaxpr/uy,myx->mux/dot_general | solution.py:43
  86.0 4.5 %fusion.255 = f32[8,256,256]{2,1,0:T(8,128)S(1)} fusion(f32[8,256,256]{2,1,0:T(8,128)S(1)} %fusion.254, f32[8,256,256]{2,1,0:T(8,128)S(1)} %fusion.248, f32[256,256]{1,0:T(8,128)S(1)} %fusion.250), kind=kOutput, calls=%fused_computation.38.clone.1 | convolution fusion | flops 1612644352 | bytes 6553600 | tf_op jit(solution)/shard_map/while/body/eval_jaxpr/uy,myx->mux/dot_general | solution.py:43
  90.5 4.9 %fusion.251 = f32[8,256,256]{2,1,0:T(8,128)S(1)} fusion(f32[8,256,256]{2,1,0:T(8,128)S(1)} %get-tuple-element.678, f32[256,256]{1,0:T(8,128)S(1)} %fusion.250), kind=kOutput, calls=%fused_computation.30.clone.1 | convolution fusion | flops 1612120064 | bytes 4456448 | tf_op jit(solution)/shard_map/while/body/eval_jaxpr/uy,myx->mux/dot_general | solution.py:46
  95.5 4.4 %fusion.252 = f32[8,256,256]{2,1,0:T(8,128)S(1)} fusion(f32[8,256,256]{2,1,0:T(8,128)S(1)} %fusion.251, f32[8,256,256]{2,1,0:T(8,128)S(1)} %fusion.248, f32[256,256]{1,0:T(8,128)S(1)} %fusion.250), kind=kOutput, calls=%fused_computation.39.clone.1 | convolution fusion | flops 1612775424 | bytes 6553600 | tf_op jit(solution)/shard_map/while/body/eval_jaxpr/uy,myx->mux/dot_general | solution.py:46
  99.9 4.3 %fusion.253 = f32[8,256,256]{2,1,0:T(8,128)S(1)} fusion(f32[8,256,256]{2,1,0:T(8,128)S(1)} %fusion.252), kind=kOutput, calls=%fused_computation.3.clone.1 | convolution fusion | flops 1611595776 | bytes 4194304 | tf_op jit(solution)/shard_map/while/body/eval_jaxpr/muy,yv->muv/dot_general | solution.py:52
  104.2 4.8 %subtract_multiply_fusion.3 = f32[8,256,256]{2,1,0:T(8,128)S(1)} fusion(f32[8,256,256]{2,1,0:T(8,128)S(1)} %get-tuple-element.676, f32[8,256,256]{2,1,0:T(8,128)S(1)} %fusion.253, f32[8,256,256]{2,1,0:T(8,128)S(1)} %fusion.255, f32[]{:T(128)S(6)} %convert_element_type.148), kind=kOutput, calls=%fused_computation.25.clone.1 | convolution fusion | flops 1613299712 | bytes 8388612 | tf_op jit(solution)/shard_map/while/body/eval_jaxpr/muy,yv->muv/dot_general | solution.py:52
  109.0 4.4 %fusion.256 = f32[8,256,256]{2,1,0:T(8,128)S(1)} fusion(f32[8,256,256]{2,1,0:T(8,128)S(1)} %fusion.252), kind=kOutput, calls=%fused_computation.5.clone.1 | convolution fusion | flops 1611726848 | bytes 4194304 | tf_op jit(solution)/shard_map/while/body/eval_jaxpr/muy,yv->muv/dot_general | solution.py:49
  113.5 6.5 %fusion.257 = (f32[8,256,256]{2,1,0:T(8,128)S(1)}, f32[8,256,256]{2,1,0:T(8,128)S(1)}, f32[256,256]{1,0:T(8,128)S(1)}, f32[256,256]{1,0:T(8,128)S(1)}) fusion(f32[8,256,256]{2,1,0:T(8,128)S(1)} %copy-done.4, f32[8,256,256]{2,1,0:T(8,128)S(1)} %subtract_multiply_fusion.3, f32[256,256]{1,0:T(8,128)S(1)} %get-tuple-element.674, ...), kind=kOutput, calls=%fused_computation.20.clone.1 | convolution fusion | flops 1622474752 | bytes 22020100 | tf_op jit(solution)/shard_map/while/body/eval_jaxpr/muy,yv->muv/dot_general | solution.py:49
  123.6 9.5 %dynamic_update_slice.11 = f32[3,512,512]{2,1,0:T(8,128)} dynamic-update-slice(f32[3,512,512]{2,1,0:T(8,128)} %get-tuple-element.704, f32[3,256,256]{2,1,0:T(8,128)S(1)} %maximum_add_fusion.2, s32[]{:T(128)} %constant.143.clone.1..sunk, s32[]{:T(128)S(6)} %select_n.177, s32[]{:T(128)S(6)} %select_n.178) | dynamic-update-slice | bytes 1572868 | tf_op jit(solution)/shard_map/while/body/eval_jaxpr/dynamic_update_slice | solution.py:102
  139.5 4.5 %fusion.247 = f32[8,256,256]{2,1,0:T(8,128)S(1)} fusion(f32[8,256,256]{2,1,0:T(8,128)S(1)} %get-tuple-element.677), kind=kOutput, calls=%fused_computation.75.clone.1 | convolution fusion | flops 1611595776 | bytes 4194304 | tf_op jit(solution)/shard_map/while/body/eval_jaxpr/uy,myx->mux/dot_general | solution.py:43
  144.1 4.4 %convolution_subtract_fusion.2 = f32[8,256,256]{2,1,0:T(8,128)S(1)} fusion(f32[8,256,256]{2,1,0:T(8,128)S(1)} %fusion.247, f32[8,256,256]{2,1,0:T(8,128)S(1)} %get-tuple-element.676), kind=kOutput, calls=%fused_computation.43.clone.1 | convolution fusion | flops 1612185600 | bytes 6291456 | tf_op jit(solution)/shard_map/while/body/eval_jaxpr/uy,myx->mux/dot_general | solution.py:43
  148.5 4.4 %fusion.245 = f32[8,256,256]{2,1,0:T(8,128)S(1)} fusion(f32[8,256,256]{2,1,0:T(8,128)S(1)} %get-tuple-element.676), kind=kOutput, calls=%fused_computation.72.clone.1 | convolution fusion | flops 1611595776 | bytes 4194304 | tf_op jit(solution)/shard_map/while/body/eval_jaxpr/uy,myx->mux/dot_general | solution.py:46
  153.0 4.5 %convolution_add_fusion.2 = f32[8,256,256]{2,1,0:T(8,128)S(1)} fusion(f32[8,256,256]{2,1,0:T(8,128)S(1)} %fusion.245, f32[8,256,256]{2,1,0:T(8,128)S(1)} %get-tuple-element.677), kind=kOutput, calls=%fused_computation.42.clone.1 | convolution fusion | flops 1612185600 | bytes 6291456 | tf_op jit(solution)/shard_map/while/body/eval_jaxpr/uy,myx->mux/dot_general | solution.py:46
  157.5 4.4 %fusion.246 = f32[8,256,256]{2,1,0:T(8,128)S(1)} fusion(f32[8,256,256]{2,1,0:T(8,128)S(1)} %convolution_add_fusion.2), kind=kOutput, calls=%fused_computation.13.clone.1 | convolution fusion | flops 1611661312 | bytes 4194304 | tf_op jit(solution)/shard_map/while/body/eval_jaxpr/muy,yv->muv/dot_general | solution.py:49
  161.9 4.7 %fusion.248 = f32[8,256,256]{2,1,0:T(8,128)S(1)} fusion(f32[8,256,256]{2,1,0:T(8,128)S(1)} %fusion.246, f32[8,256,256]{2,1,0:T(8,128)S(1)} %convolution_subtract_fusion.2), kind=kOutput, calls=%fused_computation.40.clone.1 | convolution fusion | flops 1612120064 | bytes 6291456 | tf_op jit(solution)/shard_map/while/body/eval_jaxpr/muy,yv->muv/dot_general | solution.py:49
  166.6 4.4 %fusion.249 = f32[8,256,256]{2,1,0:T(8,128)S(1)} fusion(f32[8,256,256]{2,1,0:T(8,128)S(1)} %convolution_add_fusion.2), kind=kOutput, calls=%fused_computation.11.clone.1 | convolution fusion | flops 1611595776 | bytes 4194304 | tf_op jit(solution)/shard_map/while/body/eval_jaxpr/muy,yv->muv/dot_general | solution.py:52
  171.1 4.7 %add_reduce_fusion.4 = (f32[256,256]{1,0:T(8,128)S(1)}, f32[8,256,256]{2,1,0:T(8,128)S(1)}) fusion(f32[8,256,256]{2,1,0:T(8,128)S(1)} %fusion.248, f32[8,256,256]{2,1,0:T(8,128)S(1)} %fusion.249, f32[8,256,256]{2,1,0:T(8,128)S(1)} %convolution_subtract_fusion.2), kind=kOutput, calls=%fused_computation.27.clone.1 | convolution fusion | flops 1614217216 | bytes 8650752 | tf_op jit(solution)/shard_map/while/body/eval_jaxpr/muy,yv->muv/dot_general | solution.py:52
  177.2 4.5 %fusion.254 = f32[8,256,256]{2,1,0:T(8,128)S(1)} fusion(f32[8,256,256]{2,1,0:T(8,128)S(1)} %get-tuple-element.678, f32[256,256]{1,0:T(8,128)S(1)} %fusion.250), kind=kOutput, calls=%fused_computation.32.clone.1 | convolution fusion | flops 1612251136 | bytes 4456448 | tf_op jit(solution)/shard_map/while/body/eval_jaxpr/uy,myx->mux/dot_general | solution.py:43
  181.7 4.5 %fusion.255 = f32[8,256,256]{2,1,0:T(8,128)S(1)} fusion(f32[8,256,256]{2,1,0:T(8,128)S(1)} %fusion.254, f32[8,256,256]{2,1,0:T(8,128)S(1)} %fusion.248, f32[256,256]{1,0:T(8,128)S(1)} %fusion.250), kind=kOutput, calls=%fused_computation.38.clone.1 | convolution fusion | flops 1612644352 | bytes 6553600 | tf_op jit(solution)/shard_map/while/body/eval_jaxpr/uy,myx->mux/dot_general | solution.py:43
  186.2 4.6 %fusion.251 = f32[8,256,256]{2,1,0:T(8,128)S(1)} fusion(f32[8,256,256]{2,1,0:T(8,128)S(1)} %get-tuple-element.678, f32[256,256]{1,0:T(8,128)S(1)} %fusion.250), kind=kOutput, calls=%fused_computation.30.clone.1 | convolution fusion | flops 1612120064 | bytes 4456448 | tf_op jit(solution)/shard_map/while/body/eval_jaxpr/uy,myx->mux/dot_general | solution.py:46
  190.8 4.4 %fusion.252 = f32[8,256,256]{2,1,0:T(8,128)S(1)} fusion(f32[8,256,256]{2,1,0:T(8,128)S(1)} %fusion.251, f32[8,256,256]{2,1,0:T(8,128)S(1)} %fusion.248, f32[256,256]{1,0:T(8,128)S(1)} %fusion.250), kind=kOutput, calls=%fused_computation.39.clone.1 | convolution fusion | flops 1612775424 | bytes 6553600 | tf_op jit(solution)/shard_map/while/body/eval_jaxpr/uy,myx->mux/dot_general | solution.py:46
  195.2 4.3 %fusion.253 = f32[8,256,256]{2,1,0:T(8,128)S(1)} fusion(f32[8,256,256]{2,1,0:T(8,128)S(1)} %fusion.252), kind=kOutput, calls=%fused_computation.3.clone.1 | convolution fusion | flops 1611595776 | bytes 4194304 | tf_op jit(solution)/shard_map/while/body/eval_jaxpr/muy,yv->muv/dot_general | solution.py:52
  199.5 5.0 %subtract_multiply_fusion.3 = f32[8,256,256]{2,1,0:T(8,128)S(1)} fusion(f32[8,256,256]{2,1,0:T(8,128)S(1)} %get-tuple-element.676, f32[8,256,256]{2,1,0:T(8,128)S(1)} %fusion.253, f32[8,256,256]{2,1,0:T(8,128)S(1)} %fusion.255, f32[]{:T(128)S(6)} %convert_element_type.148), kind=kOutput, calls=%fused_computation.25.clone.1 | convolution fusion | flops 1613299712 | bytes 8388612 | tf_op jit(solution)/shard_map/while/body/eval_jaxpr/muy,yv->muv/dot_general | solution.py:52
  204.6 4.4 %fusion.256 = f32[8,256,256]{2,1,0:T(8,128)S(1)} fusion(f32[8,256,256]{2,1,0:T(8,128)S(1)} %fusion.252), kind=kOutput, calls=%fused_computation.5.clone.1 | convolution fusion | flops 1611726848 | bytes 4194304 | tf_op jit(solution)/shard_map/while/body/eval_jaxpr/muy,yv->muv/dot_general | solution.py:49
  209.0 6.5 %fusion.257 = (f32[8,256,256]{2,1,0:T(8,128)S(1)}, f32[8,256,256]{2,1,0:T(8,128)S(1)}, f32[256,256]{1,0:T(8,128)S(1)}, f32[256,256]{1,0:T(8,128)S(1)}) fusion(f32[8,256,256]{2,1,0:T(8,128)S(1)} %copy-done.4, f32[8,256,256]{2,1,0:T(8,128)S(1)} %subtract_multiply_fusion.3, f32[256,256]{1,0:T(8,128)S(1)} %get-tuple-element.674, ...), kind=kOutput, calls=%fused_computation.20.clone.1 | convolution fusion | flops 1622474752 | bytes 22020100 | tf_op jit(solution)/shard_map/while/body/eval_jaxpr/muy,yv->muv/dot_general | solution.py:49
  219.2 9.2 %dynamic_update_slice.11 = f32[3,512,512]{2,1,0:T(8,128)} dynamic-update-slice(f32[3,512,512]{2,1,0:T(8,128)} %get-tuple-element.704, f32[3,256,256]{2,1,0:T(8,128)S(1)} %maximum_add_fusion.2, s32[]{:T(128)} %constant.143.clone.1..sunk, s32[]{:T(128)S(6)} %select_n.177, s32[]{:T(128)S(6)} %select_n.178) | dynamic-update-slice | bytes 1572868 | tf_op jit(solution)/shard_map/while/body/eval_jaxpr/dynamic_update_slice | solution.py:102
  235.5 4.0 pad_maximum_fusion
  239.5 6.4 %collective-permute-done.2 = f32[3,256,512]{2,1,0:T(8,128)} collective-permute-done((f32[3,256,512]{2,1,0:T(8,128)}, f32[3,256,512]{2,1,0:T(8,128)}, u32[]{:S(2)}, u32[]{:S(2)}) %collective-permute-start.2) | collective-permute-done | bytes 1572896 | tf_op jit(solution)/shard_map/ppermute | solution.py:18
  248.2 3.2 collective-permute-start.3
  251.4 22.8 %collective-permute-done.3 = f32[3,256,256]{2,1,0:T(8,128)S(1)} collective-permute-done((f32[3,256,256]{2,1,0:T(8,128)S(1)}, f32[3,256,256]{2,1,0:T(8,128)S(1)}, u32[]{:S(2)}, u32[]{:S(2)}) %collective-permute-start.3) | collective-permute-done | bytes 786464 | tf_op jit(solution)/shard_map/ppermute | solution.py:18
  274.5 19.7 %collective-permute-start.4 = (f32[2,1,256]{2,1,0:T(1,128)S(1)}, f32[2,1,256]{2,1,0:T(1,128)S(1)}, u32[]{:S(2)}, u32[]{:S(2)}) collective-permute-start(f32[2,1,256]{2,1,0:T(1,128)S(1)} %get-tuple-element.573), channel_id=1, source_target_pairs={{8,0},{16,8},{24,16},{9,1},{17,9},{25,17},{10,2},{18,10},{26,18},{... | collective-permute-start | bytes 6152 | tf_op jit(solution)/shard_map/ppermute | solution.py:29
  295.5 100.3 %all-reduce.3.cloned.1.call-done = (f32[2,8,256,256]{3,2,1,0:T(8,128)}, f32[256,256]{1,0:T(8,128)}) async-done(((f32[2,8,256,256]{3,2,1,0:T(8,128)}, f32[256,256]{1,0:T(8,128)}), (f32[2,8,256,256]{3,2,1,0:T(8,128)}, f32[256,256]{1,0:T(8,128)})) %all-reduce.3.cloned.1.call-update) | async-done | bytes 4456464 | tf_op jit(solution)/shard_map/psum | solution.py:133
  397.0 3.1 collective-permute-start.6
  402.3 6.2 %divide_add_fusion = f32[2,8,256,256]{3,2,1,0:T(8,128)} fusion(f32[2,8,256,256]{3,2,1,0:T(8,128)} %param.16, f32[2,8,256,256]{3,2,1,0:T(8,128)} %get-tuple-element.551, f32[256,256]{1,0:T(8,128)S(1)} %broadcast_add_fusion), kind=kLoop, calls=%fused_computation.171 | loop fusion | flops 2097152 | bytes 12845056 | tf_op jit(solution)/shard_map/add | solution.py:134
  408.5 3.3 collective-permute-done.7
  (69 shorter events, 40.9 us)
Async XLA Ops:
  7.2 388.7 %all-reduce.3.cloned.1.call-start = ((), (), s32[]{:S(2)}) async-start(), calls=%async_computation | async-start | bytes 8912896 | tf_op jit(solution)/shard_map/psum | solution.py:133
  7.2 14.9 %collective-permute-start = (f32[2,256,256]{2,1,0:T(8,128)}, f32[2,256,256]{2,1,0:T(8,128)S(1)}, u32[]{:S(2)}, u32[]{:S(2)}) collective-permute-start(f32[2,256,256]{2,1,0:T(8,128)} %param.15), channel_id=1, source_target_pairs={{1,0},{2,1},{3,2},{4,3},{5,4},{6,5},{7,6},{9,8},{10,9},{11,10},{12... | collective-permute-start | bytes 1572872 | tf_op jit(solution)/shard_map/ppermute | solution.py:18
  23.0 9.6 %collective-permute-start.1 = (f32[2,256,512]{2,1,0:T(8,128)}, f32[2,256,512]{2,1,0:T(8,128)}, u32[]{:S(2)}, u32[]{:S(2)}) collective-permute-start(f32[2,256,512]{2,1,0:T(8,128)} %constant_dynamic-update-slice_fusion), channel_id=1, source_target_pairs={{8,0},{16,8},{24,16},{9,1},{17,9},{25,17},{10,2},{18,10},{26,18},{... | collective-permute-start | bytes 3145736 | tf_op jit(solution)/shard_map/ppermute | solution.py:18
  27.5 3.4 copy-start.6
  35.7 2.1 copy-start.9
  104.2 9.3 %copy-start.4 = (f32[8,256,256]{2,1,0:T(8,128)S(1)}, f32[8,256,256]{2,1,0:T(8,128)}, u32[]{:S(2)}) copy-start(f32[8,256,256]{2,1,0:T(8,128)} %get-tuple-element.706) | copy-start | bytes 6291460 | tf_op jit(solution)/shard_map/while
  109.0 4.5 %copy-start = (f32[8,256,256]{2,1,0:T(8,128)S(1)}, f32[8,256,256]{2,1,0:T(8,128)}, u32[]{:S(2)}) copy-start(f32[8,256,256]{2,1,0:T(8,128)} %get-tuple-element.730) | copy-start | bytes 6291460 | tf_op jit(solution)/shard_map/while
  109.0 4.5 %copy-start.1 = (f32[8,256,256]{2,1,0:T(8,128)S(1)}, f32[8,256,256]{2,1,0:T(8,128)}, u32[]{:S(2)}) copy-start(f32[8,256,256]{2,1,0:T(8,128)} %get-tuple-element.705) | copy-start | bytes 6291460 | tf_op jit(solution)/shard_map/while
  120.0 1.3 copy-start.2
  120.0 2.1 copy-start.5
  199.5 9.5 %copy-start.4 = (f32[8,256,256]{2,1,0:T(8,128)S(1)}, f32[8,256,256]{2,1,0:T(8,128)}, u32[]{:S(2)}) copy-start(f32[8,256,256]{2,1,0:T(8,128)} %get-tuple-element.706) | copy-start | bytes 6291460 | tf_op jit(solution)/shard_map/while
  204.6 4.5 %copy-start = (f32[8,256,256]{2,1,0:T(8,128)S(1)}, f32[8,256,256]{2,1,0:T(8,128)}, u32[]{:S(2)}) copy-start(f32[8,256,256]{2,1,0:T(8,128)} %get-tuple-element.730) | copy-start | bytes 6291460 | tf_op jit(solution)/shard_map/while
  204.6 4.5 %copy-start.1 = (f32[8,256,256]{2,1,0:T(8,128)S(1)}, f32[8,256,256]{2,1,0:T(8,128)}, u32[]{:S(2)}) copy-start(f32[8,256,256]{2,1,0:T(8,128)} %get-tuple-element.705) | copy-start | bytes 6291460 | tf_op jit(solution)/shard_map/while
  215.5 1.3 copy-start.2
  215.5 2.1 copy-start.5
  231.3 8.2 %copy-start.7 = (f32[256,256]{1,0:T(8,128)}, f32[256,256]{1,0:T(8,128)S(1)}, u32[]{:S(2)}) copy-start(f32[256,256]{1,0:T(8,128)S(1)} %get-tuple-element.415) | copy-start | bytes 786436
  231.3 4.1 copy-start.3
  234.2 11.7 %collective-permute-start.2 = (f32[3,256,512]{2,1,0:T(8,128)}, f32[3,256,512]{2,1,0:T(8,128)}, u32[]{:S(2)}, u32[]{:S(2)}) collective-permute-start(f32[3,256,512]{2,1,0:T(8,128)} %slice.119), channel_id=1, source_target_pairs={{0,8},{8,16},{16,24},{1,9},{9,17},{17,25},{2,10},{10,18},{18,26},{... | collective-permute-start | bytes 4718600 | tf_op jit(solution)/shard_map/ppermute | solution.py:18
  248.1 26.3 %copy-start.8 = (f32[2,256,256]{2,1,0:T(8,128)S(1)}, f32[2,256,256]{2,1,0:T(8,128)}, u32[]{:S(2)}) copy-start(f32[2,256,256]{2,1,0:T(8,128)} %param.15) | copy-start | bytes 1572868
  248.2 26.0 %collective-permute-start.3 = (f32[3,256,256]{2,1,0:T(8,128)S(1)}, f32[3,256,256]{2,1,0:T(8,128)S(1)}, u32[]{:S(2)}, u32[]{:S(2)}) collective-permute-start(f32[3,256,256]{2,1,0:T(8,128)S(1)} %slice.139), channel_id=1, source_target_pairs={{0,1},{1,2},{2,3},{3,4},{4,5},{5,6},{6,7},{8,9},{9,10},{10,11},{11... | collective-permute-start | bytes 2359304 | tf_op jit(solution)/shard_map/ppermute | solution.py:18
  274.5 122.3 %collective-permute-start.4 = (f32[2,1,256]{2,1,0:T(1,128)S(1)}, f32[2,1,256]{2,1,0:T(1,128)S(1)}, u32[]{:S(2)}, u32[]{:S(2)}) collective-permute-start(f32[2,1,256]{2,1,0:T(1,128)S(1)} %get-tuple-element.573), channel_id=1, source_target_pairs={{8,0},{16,8},{24,16},{9,1},{17,9},{25,17},{10,2},{18,10},{26,18},{... | collective-permute-start | bytes 6152 | tf_op jit(solution)/shard_map/ppermute | solution.py:29
  294.2 102.6 %collective-permute-start.5 = (f32[2,1,256]{2,1,0:T(1,128)S(1)}, f32[2,1,256]{2,1,0:T(1,128)S(1)}, u32[]{:S(2)}, u32[]{:S(2)}) collective-permute-start(f32[2,1,256]{2,1,0:T(1,128)S(1)} %get-tuple-element.572), channel_id=1, source_target_pairs={{0,8},{8,16},{16,24},{1,9},{9,17},{17,25},{2,10},{10,18},{18,26},{... | collective-permute-start | bytes 6152 | tf_op jit(solution)/shard_map/ppermute | solution.py:28
  397.0 11.5 %collective-permute-start.6 = (f32[2,258,1]{2,1,0:T(8,128)S(1)}, f32[2,258,1]{2,1,0:T(8,128)S(1)}, u32[]{:S(2)}, u32[]{:S(2)}) collective-permute-start(f32[2,258,1]{2,1,0:T(8,128)S(1)} %get-tuple-element.570), channel_id=1, source_target_pairs={{1,0},{2,1},{3,2},{4,3},{5,4},{6,5},{7,6},{9,8},{10,9},{11,10},{12... | collective-permute-start | bytes 6200 | tf_op jit(solution)/shard_map/ppermute | solution.py:29
  400.1 11.6 %collective-permute-start.7 = (f32[2,258,1]{2,1,0:T(8,128)S(1)}, f32[2,258,1]{2,1,0:T(8,128)S(1)}, u32[]{:S(2)}, u32[]{:S(2)}) collective-permute-start(f32[2,258,1]{2,1,0:T(8,128)S(1)} %get-tuple-element.571), channel_id=1, source_target_pairs={{0,1},{1,2},{2,3},{3,4},{4,5},{5,6},{6,7},{8,9},{9,10},{10,11},{11... | collective-permute-start | bytes 6200 | tf_op jit(solution)/shard_map/ppermute | solution.py:28
Sparse Core Ops, SparseCore 0:
  239.6 156.1 all-reduce.2
where the time goes:
time: 427 us; the launch traced here: 420 us
  matrix products  149 us (35%)
  waiting for transfers between devices  143 us (33%)
  starting transfers between devices  38.3 us (9%)
  local copies, waits for them, and re-layouts  34.5 us (8%)
  other arithmetic  33.5 us (8%)
  between operations  14.4 us (3%)
  loops' own time  7.45 us (2%)
    psum x1, waiting for transfers between devices, per_device(): gradient_all, power_all = lax.psum((gradient, object_power), ('row', 'col'))  100 us
    ppermute x4, waiting for transfers between devices, shifted(): lax.ppermute(value, axis, [(source, source + steps) for source in range(f...  39.1 us
    ppermute x2, starting transfers between devices, extended_2(): after = lax.ppermute(first, axis, down)  22.9 us
    dot_general x4, matrix products, transform(): jnp.einsum('muy,yv->muv', left_real, table_real, precision=HIGHEST)  22.4 us
    dot_general x4, matrix products, transform(): jnp.einsum('muy,yv->muv', left_real, table_imag, precision=HIGHEST)  19.2 us
    dot_general x4, matrix products, transform(): jnp.einsum('uy,myx->mux', table_real, field_imag, precision=HIGHEST)  18.8 us
    dynamic_update_slice x2, local copies, waits for them, and re-layouts, update_slot(): lax.dynamic_update_slice(totals, current + addition, (zero_index, row_sta...  18.7 us
    dot_general x4, matrix products, transform(): jnp.einsum('uy,myx->mux', table_real, field_real, precision=HIGHEST)  18.1 us
  transfers between devices with their start and end apart: 9, of which 5 were waited for; matrix products, arithmetic and copies ran while one was open for 5% of the time, Pallas kernels for 0%

commit v1 on v0

v1 whole, which is shorter than its diff:
```python
import functools
import math

import jax
import jax.numpy as jnp
import ml_dtypes
import numpy as np
from jax import lax
from jax.experimental import pallas as pl
from jax.experimental.pallas import tpu as pltpu
from jax.sharding import PartitionSpec as P

INTENSITY_FLOOR = 0.1
OBJECT_DELTA = 0.5
PROBE_DELTA = 1.0
SMOOTH_WEIGHT = 0.1
F32 = jnp.float32
BF16 = jnp.bfloat16


def tables(frame):
    half = frame // 2
    n = np.arange(half)
    angle = -2.0 * np.pi * (np.outer(n, n) % half) / half
    c, s = np.cos(angle) / math.sqrt(frame), np.sin(angle) / math.sqrt(frame)
    full = np.block([[c, s], [-s, c]]).astype(np.float32)
    high = full.astype(ml_dtypes.bfloat16)
    low = (full - high.astype(np.float32)).astype(ml_dtypes.bfloat16)
    right_f = np.concatenate([high, high, low], axis=0)
    right_i = np.concatenate([high.T, high.T, low.T], axis=0)
    left_f = np.concatenate([high.T, high.T, low.T], axis=1)
    left_i = np.concatenate([high, high, low], axis=1)
    turn = -2.0 * np.pi * n / frame
    tw = np.stack([np.cos(turn), np.sin(turn)]).astype(np.float32)
    rows = np.broadcast_to(tw[:, None, :], (2, 8, half)).copy()
    cols = np.broadcast_to(tw[:, :, None], (2, half, frame)).copy()
    return right_f, right_i, left_f, left_i, rows, cols


def split(x):
    high = x.astype(BF16)
    return high, (x - high.astype(F32)).astype(BF16)


def right_dot(x, table):
    high, low = split(x)
    return jnp.dot(jnp.concatenate([high, low, high], axis=1), table, preferred_element_type=F32)


def left_dot(table, x):
    high, low = split(x)
    return jnp.dot(table, jnp.concatenate([high, low, high], axis=0), preferred_element_type=F32)


def waves_kernel(
    place, live, own, right, down, diag, probe, amplitude, rf, ri, lf, li, twr, twc,
    totals, grad, power, spectra, ratio, accum,
):
    modes, frame = probe.shape[1], probe.shape[2]
    half = frame // 2
    slots = amplitude.shape[0]
    tile = own.shape[1]
    cat = jnp.concatenate

    for slot in range(slots):
        row, col = place[0, slot], place[1, slot]
        flag = live[slot].astype(F32)
        height, width = 2 * tile, 2 * tile
        patch = []
        for part in range(2):
            whole = cat(
                [cat([own[part], right[part]], axis=1), cat([down[part], diag[part]], axis=1)], axis=0
            )
            whole = pltpu.roll(whole, lax.rem(height - row, height), 0)[:frame]
            patch.append(pltpu.roll(whole, lax.rem(width - col, width), 1)[:, :frame])
        qr, qi = patch
        accum[0], accum[1] = qr, qi
        accum[2] = jnp.zeros((frame, frame), F32)

        @pl.loop(0, modes)
        def _(m):
            qr, qi, pr, pi = accum[0], accum[1], probe[0, m], probe[1, m]
            wr, wi = pr * qr - pi * qi, pr * qi + pi * qr
            c, s = twr[0, 0:1], twr[1, 0:1]
            dr, di = wr[:, :half] - wr[:, half:], wi[:, :half] - wi[:, half:]
            x = cat(
                [
                    cat([wr[:, :half] + wr[:, half:], wi[:, :half] + wi[:, half:]], axis=1),
                    cat([dr * c - di * s, dr * s + di * c], axis=1),
                ],
                axis=0,
            )
            y = right_dot(x, rf[...])
            yr = cat([y[:frame, :half], y[frame:, :half]], axis=1)
            yi = cat([y[:frame, half:], y[frame:, half:]], axis=1)
            c, s = twc[0], twc[1]
            dr, di = yr[:half] - yr[half:], yi[:half] - yi[half:]
            z = cat(
                [
                    cat([yr[:half] + yr[half:], yi[:half] + yi[half:]], axis=0),
                    cat([dr * c - di * s, dr * s + di * c], axis=0),
                ],
                axis=1,
            )
            r = left_dot(lf[...], z)
            spectra[m] = r
            accum[2] += cat(
                [
                    r[:half, :frame] * r[:half, :frame] + r[half:, :frame] * r[half:, :frame],
                    r[:half, frame:] * r[:half, frame:] + r[half:, frame:] * r[half:, frame:],
                ],
                axis=0,
            )

        scale = amplitude[slot] * lax.rsqrt(jnp.maximum(accum[2], INTENSITY_FLOOR))
        ratio[:half, :frame] = scale[:half]
        ratio[half:, :frame] = scale[:half]
        ratio[:half, frame:] = scale[half:]
        ratio[half:, frame:] = scale[half:]
        for part in range(3):
            accum[2 + part] = jnp.zeros((frame, frame), F32)

        @pl.loop(0, modes)
        def _(m):
            r = left_dot(li[...], spectra[m] * ratio[...])
            c, s = twc[0], twc[1]
            er, ei, dr, di = r[:half, :frame], r[half:, :frame], r[:half, frame:], r[half:, frame:]
            vr, vi = dr * c + di * s, di * c - dr * s
            yr = cat([er + vr, er - vr], axis=0)
            yi = cat([ei + vi, ei - vi], axis=0)
            x = cat(
                [cat([yr[:, :half], yi[:, :half]], axis=1), cat([yr[:, half:], yi[:, half:]], axis=1)],
                axis=0,
            )
            y = right_dot(x, ri[...])
            c, s = twr[0, 0:1], twr[1, 0:1]
            er, ei, dr, di = y[:frame, :half], y[:frame, half:], y[frame:, :half], y[frame:, half:]
            vr, vi = dr * c + di * s, di * c - dr * s
            qr, qi, pr, pi = accum[0], accum[1], probe[0, m], probe[1, m]
            br = (cat([er + vr, er - vr], axis=1) - (pr * qr - pi * qi)) * flag
            bi = (cat([ei + vi, ei - vi], axis=1) - (pr * qi + pi * qr)) * flag
            accum[2] += pr * br + pi * bi
            accum[3] += pr * bi - pi * br
            accum[4] += flag * (pr * pr + pi * pi)
            gr, gi = qr * br + qi * bi, qr * bi - qi * br
            if slot == 0:
                grad[0, m], grad[1, m] = gr, gi
            else:
                grad[0, m] += gr
                grad[1, m] += gi

        strength = flag * (qr * qr + qi * qi)
        power[...] = strength if slot == 0 else power[...] + strength
        for part in range(3):
            piece = accum[2 + part]
            piece = cat([piece, jnp.zeros((frame, width - frame), F32)], axis=1)
            piece = pltpu.roll(piece, col, 1)
            piece = cat([piece, jnp.zeros((height - frame, width), F32)], axis=0)
            piece = pltpu.roll(piece, row, 0)
            totals[part] = piece if slot == 0 else totals[part] + piece


def waves(place, live, own, right, down, diag, probe, amplitude):
    modes, frame = probe.shape[1], probe.shape[2]
    tile = own.shape[1]
    smem = pl.BlockSpec(memory_space=pltpu.SMEM)
    vmem = pl.BlockSpec(memory_space=pltpu.VMEM)
    return pl.pallas_call(
        waves_kernel,
        out_shape=(
            jax.ShapeDtypeStruct((3, 2 * tile, 2 * tile), F32),
            jax.ShapeDtypeStruct(probe.shape, F32),
            jax.ShapeDtypeStruct((frame, frame), F32),
        ),
        in_specs=[smem] * 2 + [vmem] * 12,
        out_specs=(vmem, vmem, vmem),
        scratch_shapes=[
            pltpu.VMEM((modes, frame, 2 * frame), F32),
            pltpu.VMEM((frame, 2 * frame), F32),
            pltpu.VMEM((5, frame, frame), F32),
        ],
        compiler_params=pltpu.CompilerParams(vmem_limit_bytes=48 << 20),
        cost_estimate=pl.CostEstimate(
            flops=60_000_000_000, bytes_accessed=16 << 20, transcendentals=0
        ),
    )(place, live, own, right, down, diag, probe, amplitude, *tables(frame))


def moved(value, down, right):
    rows, cols = lax.axis_size("row"), lax.axis_size("col")
    pairs = [
        (r * cols + c, (r + down) * cols + c + right)
        for r in range(rows)
        for c in range(cols)
        if 0 <= r + down < rows and 0 <= c + right < cols
    ]
    return lax.ppermute(value, ("row", "col"), pairs)


def per_device(object_field, probe_modes, patterns, offsets, counts):
    tile, frame = object_field.shape[1], probe_modes.shape[-1]
    slots = patterns.shape[0]
    right = moved(object_field, 0, -1)
    down = moved(object_field, -1, 0)
    diag = moved(object_field, -1, -1)
    base = jnp.stack([lax.axis_index("row"), lax.axis_index("col")]).astype(jnp.int32) * tile
    place = offsets - base[:, None]
    live = (jnp.arange(slots, dtype=jnp.int32) < counts[0]).astype(jnp.int32)
    half = frame // 2
    amplitude = patterns.reshape(slots, half, 2, half, 2).transpose(0, 2, 1, 4, 3)
    amplitude = amplitude.reshape(slots, frame, frame)
    totals, gradient, power = waves(
        place, live, object_field, right, down, diag, probe_modes, amplitude
    )
    gradient_all, power_all = lax.psum((gradient, power), ("row", "col"))
    sums = totals[:, :tile, :tile] + moved(totals[:, :tile, tile:], 0, 1)
    sums = sums + moved(totals[:, tile:, :tile], 1, 0) + moved(totals[:, tile:, tile:], 1, 1)
    updated = object_field + sums[:2] / (sums[2] + OBJECT_DELTA)
    above = moved(updated[:, -1, :], 1, 0)
    below = moved(updated[:, 0, :], -1, 0)
    before = moved(updated[:, :, -1], 0, 1)
    after = moved(updated[:, :, 0], 0, -1)
    neighbours = (
        jnp.concatenate([updated[:, 1:], below[:, None]], axis=1)
        + jnp.concatenate([above[:, None], updated[:, :-1]], axis=1)
        + jnp.concatenate([updated[:, :, 1:], after[:, :, None]], axis=2)
        + jnp.concatenate([before[:, :, None], updated[:, :, :-1]], axis=2)
    )
    new_object = updated + SMOOTH_WEIGHT * (neighbours - 4.0 * updated)
    new_probe = probe_modes + gradient_all / (power_all[None, None] + PROBE_DELTA)
    return (new_object, new_probe)


def solution(mesh):
    return jax.shard_map(
        per_device,
        mesh=mesh,
        in_specs=(
            P(None, "row", "col"),
            P(),
            P(("row", "col"), None, None),
            P(None, ("row", "col")),
            P(("row", "col")),
        ),
        out_specs=(P(None, "row", "col"), P()),
        check_vma=False,
    )
```

time: 427 us -> 305 us (0.71)
  matrix products: 149 us -> 0 us
  Pallas kernels: 0 us -> 43.9 us
  local copies, waits for them, and re-layouts: 34.5 us -> 61.1 us
  other arithmetic: 33.5 us -> 10.6 us
  starting transfers between devices: 38.3 us -> 30.5 us
  loops' own time: 7.45 us -> 0 us
    dot_general x32 -> x0, matrix products: 149 us -> none  [the longest x4 22.4 us: transform(): jnp.einsum('muy,yv->muv', left_real, table_real, precision=HIGHEST)]
    pallas_call x0 -> x1, Pallas kernels: none -> 43.9 us  [waves(): pl.pallas_call(waves_kernel, out_shape=(jax.ShapeDtypeStruct((3, 2 * tile...]
    reshape x0 -> x2, local copies, waits for them, and re-layouts: none -> 37.1 us  [the longest x1 35.6 us: per_device(): patterns.reshape(slots, half, 2, half, 2).transpose(0, 2, 1, 4, 3)]
    dynamic_update_slice x2 -> x0, local copies, waits for them, and re-layouts: 18.7 us -> none  [update_slot(): lax.dynamic_update_slice(totals, current + addition, (zero_index, row_sta...]
    transpose x0 -> x1, local copies, waits for them, and re-layouts: none -> 18.3 us  [per_device(): patterns.reshape(slots, half, 2, half, 2).transpose(0, 2, 1, 4, 3)]
    psum x1, waiting for transfers between devices: 100 us -> 92.3 us  [per_device(): gradient_all, power_all = lax.psum((gradient, power), ('row', 'col'))]
    ppermute x8 -> x10, starting transfers between devices: 38.2 us -> 30.5 us  [moved(): return lax.ppermute(value, ('row', 'col'), pairs)]
    another operation x1 -> x0, loops' own time: 7.45 us -> none  [per_device(): lax.fori_loop(0, slot_count, update_slot, initial)]
  transfers between devices with their start and end apart: 9 -> 11, of which waited for: 5 -> 4; matrix products, arithmetic and copies ran while one was open for 5% -> 20% of each run, Pallas kernels for 0% -> 0%
where the time goes in v1:
time: 305 us; the launch traced here: 301 us
  waiting for transfers between devices  140 us (46%)
  local copies, waits for them, and re-layouts  61.1 us (20%)
  Pallas kernels  43.9 us (14%)
  starting transfers between devices  30.5 us (10%)
  between operations  14.9 us (5%)
  other arithmetic  10.6 us (3%)
    psum x1, waiting for transfers between devices, per_device(): gradient_all, power_all = lax.psum((gradient, power), ('row', 'col'))  92.3 us
    ppermute x10, waiting for transfers between devices, moved(): return lax.ppermute(value, ('row', 'col'), pairs)  47.2 us
    pallas_call x1, Pallas kernels, waves(): pl.pallas_call(waves_kernel, out_shape=(jax.ShapeDtypeStruct((3, 2 * tile...  43.9 us
    reshape x1, local copies, waits for them, and re-layouts, per_device(): patterns.reshape(slots, half, 2, half, 2).transpose(0, 2, 1, 4, 3)  35.6 us
    ppermute x10, starting transfers between devices, moved(): return lax.ppermute(value, ('row', 'col'), pairs)  30.5 us
    transpose x1, local copies, waits for them, and re-layouts, per_device(): patterns.reshape(slots, half, 2, half, 2).transpose(0, 2, 1, 4, 3)  18.3 us
    add x1, other arithmetic, per_device(): probe_modes + gradient_all / (power_all[None, None] + PROBE_DELTA)  6.16 us
  transfers between devices with their start and end apart: 11, of which 4 were waited for; matrix products, arithmetic and copies ran while one was open for 20% of the time, Pallas kernels for 0%

profile of v1, /device:TPU:13, one launch (start us, length us, event | category | flops | bytes accessed | tf_op | source)
XLA Modules:
  0.0 300.6 jit_solution(589692678543393725)
XLA Ops:
  7.2 0.0 all-reduce.3.cloned.1.call-start
  7.2 3.0 %collective-permute-start = (f32[2,256,256]{2,1,0:T(8,128)}, f32[2,256,256]{2,1,0:T(8,128)S(1)}, u32[]{:S(2)}, u32[]{:S(2)}) collective-permute-start(f32[2,256,256]{2,1,0:T(8,128)} %own.1), channel_id=1, source_target_pairs={{1,0},{2,1},{3,2},{4,3},{5,4},{6,5},{7,6},{9,8},{10,9},{11,10},{12... | collective-permute-start | bytes 1572872 | tf_op jit(solution)/shard_map/ppermute | solution.py:197
  10.2 2.9 collective-permute-start.1
  13.1 2.1 collective-permute-start.2
  15.2 35.6 %reshape.29 = f32[2,128,2,128,2]{4,3,2,1,0:T(8,128)} reshape(f32[2,256,256]{2,1,0:T(8,128)} %param.13) | data formatting | bytes 1048576 | tf_op jit(solution)/shard_map/reshape | solution.py:210
  50.8 0.0 copy-start.6
  50.8 18.3 %copy.23 = f32[2,2,128,2,128]{4,3,2,1,0:T(2,128)} copy(f32[2,2,128,2,128]{3,4,1,2,0:T(8,128)} %bitcast.15) | data formatting | bytes 1048576 | tf_op jit(solution)/shard_map/transpose | solution.py:210
  69.2 1.5 reshape.30.amplitude
  71.3 0.1 add_multiply_fusion
  71.4 0.0 copy-done.7
  71.4 0.1 broadcast_subtract_fusion.place
  71.5 0.0 collective-permute-done.right
  71.5 0.0 collective-permute-done.1.down
  71.5 0.0 collective-permute-done.2.diag
  71.5 0.0 copy-done
  71.5 0.0 copy-done.1
  71.5 0.0 copy-start.3
  71.5 1.0 copy-done.3
  72.5 1.0 copy-done.4
  73.5 0.9 copy-done.5
  74.5 43.9 %shard_map.122 = (f32[3,512,512]{2,1,0:T(8,128)}, f32[2,8,256,256]{3,2,1,0:T(8,128)}, f32[256,256]{1,0:T(8,128)}) custom-call(s32[2,2]{1,0:T(2,128)S(1)} %broadcast_subtract_fusion.place, s32[2]{0:T(128)S(1)} %compare_convert_fusion.live, f32[2,256,256]{2,1,0:T(8,128)S(1)} %copy-done, f32[2,256,256]{2,1,0:T(8,128)S(1)} %collective-permute-done.right, ...), custom_call_target="tpu_custom_call" | custom-call | flops 60000002048 | bytes 16777216 | tf_op jit(solution)/shard_map/pallas_call | solution.py:168
  118.3 1.9 fusion.7
  120.2 3.1 %collective-permute-start.3 = (f32[3,256,256]{2,1,0:T(8,128)S(1)}, f32[3,256,256]{2,1,0:T(8,128)}, u32[]{:S(2)}, u32[]{:S(2)}) collective-permute-start(f32[3,256,256]{2,1,0:T(8,128)S(1)} %get-tuple-element.12), channel_id=1, source_target_pairs={{0,1},{1,2},{2,3},{3,4},{4,5},{5,6},{6,7},{8,9},{9,10},{10,11},{11... | collective-permute-start | bytes 2359304 | tf_op jit(solution)/shard_map/ppermute | solution.py:197
  123.3 1.3 collective-permute-start.4
  124.6 1.3 collective-permute-start.5
  125.9 0.0 all-reduce.3.cloned.1.call-update
  125.9 20.5 %collective-permute-done.3 = f32[3,256,256]{2,1,0:T(8,128)} collective-permute-done((f32[3,256,256]{2,1,0:T(8,128)S(1)}, f32[3,256,256]{2,1,0:T(8,128)}, u32[]{:S(2)}, u32[]{:S(2)}) %collective-permute-start.3) | collective-permute-done | bytes 786464 | tf_op jit(solution)/shard_map/ppermute | solution.py:197
  146.4 0.0 collective-permute-done.4
  146.4 25.6 %collective-permute-done.5 = f32[3,256,256]{2,1,0:T(8,128)} collective-permute-done((f32[3,256,256]{2,1,0:T(8,128)S(1)}, f32[3,256,256]{2,1,0:T(8,128)}, u32[]{:S(2)}, u32[]{:S(2)}) %collective-permute-start.5) | collective-permute-done | bytes 786464 | tf_op jit(solution)/shard_map/ppermute | solution.py:197
  172.0 2.1 add_add_fusion
  174.1 0.1 fusion
  174.2 0.3 slice_reduce_fusion
  174.5 1.9 collective-permute-start.8
  176.4 3.4 %collective-permute-start.9 = (f32[2,256]{1,0:T(2,128)S(1)}, f32[2,256]{1,0:T(2,128)S(1)}, u32[]{:S(2)}, u32[]{:S(2)}) collective-permute-start(f32[2,256]{1,0:T(2,128)S(1)} %get-tuple-element.8), channel_id=1, source_target_pairs={{0,1},{1,2},{2,3},{3,4},{4,5},{5,6},{6,7},{8,9},{9,10},{10,11},{11... | collective-permute-start | bytes 6152 | tf_op jit(solution)/shard_map/ppermute | solution.py:197
  179.8 10.3 %collective-permute-start.6 = (f32[2,256]{1,0:T(2,128)S(1)}, f32[2,256]{1,0:T(2,128)S(1)}, u32[]{:S(2)}, u32[]{:S(2)}) collective-permute-start(f32[2,256]{1,0:T(2,128)S(1)} %bitcast.18), channel_id=1, source_target_pairs={{8,0},{9,1},{10,2},{11,3},{12,4},{13,5},{14,6},{15,7},{16,8},{17,9... | collective-permute-start | bytes 6152 | tf_op jit(solution)/shard_map/ppermute | solution.py:197
  190.1 1.3 collective-permute-start.7
  191.4 0.2 fusion.8
  191.6 0.1 fusion.10
  191.7 0.0 collective-permute-done.8
  191.7 0.1 copy.26
  191.9 0.0 collective-permute-done.9
  191.9 0.1 copy.27
  192.0 0.0 collective-permute-done.6
  192.1 1.1 collective-permute-done.7
  193.2 1.1 fusion.5
  194.3 92.3 %all-reduce.3.cloned.1.call-done = (f32[2,8,256,256]{3,2,1,0:T(8,128)}, f32[256,256]{1,0:T(8,128)}) async-done(((f32[2,8,256,256]{3,2,1,0:T(8,128)}, f32[256,256]{1,0:T(8,128)}), (f32[2,8,256,256]{3,2,1,0:T(8,128)}, f32[256,256]{1,0:T(8,128)})) %all-reduce.3.cloned.1.call-update) | async-done | bytes 4456464 | tf_op jit(solution)/shard_map/psum | solution.py:215
  286.6 1.0 broadcast_add_fusion
  287.6 6.2 %divide_add_fusion = f32[2,8,256,256]{3,2,1,0:T(8,128)} fusion(f32[2,8,256,256]{3,2,1,0:T(8,128)} %probe.1, f32[2,8,256,256]{3,2,1,0:T(8,128)} %get-tuple-element.10, f32[256,256]{1,0:T(8,128)S(1)} %broadcast_add_fusion), kind=kLoop, calls=%fused_computation | loop fusion | flops 2097152 | bytes 12845056 | tf_op jit(solution)/shard_map/add | solution.py:230
  (15 shorter events, 0.1 us)
Async XLA Ops:
  7.2 279.5 %all-reduce.3.cloned.1.call-start = ((), (), s32[]{:S(2)}) async-start(), calls=%async_computation | async-start | bytes 8912896 | tf_op jit(solution)/shard_map/psum | solution.py:215
  7.2 64.2 %collective-permute-start = (f32[2,256,256]{2,1,0:T(8,128)}, f32[2,256,256]{2,1,0:T(8,128)S(1)}, u32[]{:S(2)}, u32[]{:S(2)}) collective-permute-start(f32[2,256,256]{2,1,0:T(8,128)} %own.1), channel_id=1, source_target_pairs={{1,0},{2,1},{3,2},{4,3},{5,4},{6,5},{7,6},{9,8},{10,9},{11,10},{12... | collective-permute-start | bytes 1572872 | tf_op jit(solution)/shard_map/ppermute | solution.py:197
  10.2 61.2 %collective-permute-start.1 = (f32[2,256,256]{2,1,0:T(8,128)}, f32[2,256,256]{2,1,0:T(8,128)S(1)}, u32[]{:S(2)}, u32[]{:S(2)}) collective-permute-start(f32[2,256,256]{2,1,0:T(8,128)} %own.1), channel_id=1, source_target_pairs={{8,0},{9,1},{10,2},{11,3},{12,4},{13,5},{14,6},{15,7},{16,8},{17,9... | collective-permute-start | bytes 1572872 | tf_op jit(solution)/shard_map/ppermute | solution.py:197
  13.1 58.3 %collective-permute-start.2 = (f32[2,256,256]{2,1,0:T(8,128)}, f32[2,256,256]{2,1,0:T(8,128)S(1)}, u32[]{:S(2)}, u32[]{:S(2)}) collective-permute-start(f32[2,256,256]{2,1,0:T(8,128)} %own.1), channel_id=1, source_target_pairs={{9,0},{10,1},{11,2},{12,3},{13,4},{14,5},{15,6},{17,8},{18,9},{19,... | collective-permute-start | bytes 1572872 | tf_op jit(solution)/shard_map/ppermute | solution.py:197
  50.8 20.6 %copy-start.7 = (s32[2,2]{1,0:T(2,128)S(1)}, s32[2,2]{1,0:T(2,128)}, u32[]{:S(2)}) copy-start(s32[2,2]{1,0:T(2,128)} %param.14) | copy-start | bytes 52
  50.8 20.7 %copy-start = (f32[2,256,256]{2,1,0:T(8,128)S(1)}, f32[2,256,256]{2,1,0:T(8,128)}, u32[]{:S(2)}) copy-start(f32[2,256,256]{2,1,0:T(8,128)} %own.1) | copy-start | bytes 1572868
  50.8 20.7 %copy-start.1 = (bf16[768,256]{1,0:T(8,128)(2,1)S(1)}, bf16[768,256]{1,0:T(8,128)(2,1)}, u32[]{:S(2)}) copy-start(bf16[768,256]{1,0:T(8,128)(2,1)} %constant.30.clone.rf) | copy-start | bytes 1179652
  50.8 20.7 %copy-start.2 = (bf16[768,256]{1,0:T(8,128)(2,1)S(1)}, bf16[768,256]{1,0:T(8,128)(2,1)}, u32[]{:S(2)}) copy-start(bf16[768,256]{1,0:T(8,128)(2,1)} %constant.31.clone.ri) | copy-start | bytes 1179652
  50.8 20.7 %copy-start.6 = (f32[2,8,128]{2,1,0:T(8,128)S(1)}, f32[2,8,128]{2,1,0:T(8,128)}, u32[]{:S(2)}) copy-start(f32[2,8,128]{2,1,0:T(8,128)} %constant.34.clone.twr) | copy-start | bytes 24580
  71.5 1.0 copy-start.3
  72.5 1.0 copy-start.4
  73.5 0.9 copy-start.5
  120.2 26.2 %collective-permute-start.3 = (f32[3,256,256]{2,1,0:T(8,128)S(1)}, f32[3,256,256]{2,1,0:T(8,128)}, u32[]{:S(2)}, u32[]{:S(2)}) collective-permute-start(f32[3,256,256]{2,1,0:T(8,128)S(1)} %get-tuple-element.12), channel_id=1, source_target_pairs={{0,1},{1,2},{2,3},{3,4},{4,5},{5,6},{6,7},{8,9},{9,10},{10,11},{11... | collective-permute-start | bytes 2359304 | tf_op jit(solution)/shard_map/ppermute | solution.py:197
  123.3 23.1 %collective-permute-start.4 = (f32[3,256,256]{2,1,0:T(8,128)S(1)}, f32[3,256,256]{2,1,0:T(8,128)}, u32[]{:S(2)}, u32[]{:S(2)}) collective-permute-start(f32[3,256,256]{2,1,0:T(8,128)S(1)} %get-tuple-element.14), channel_id=1, source_target_pairs={{0,8},{1,9},{2,10},{3,11},{4,12},{5,13},{6,14},{7,15},{8,16},{9,17... | collective-permute-start | bytes 2359304 | tf_op jit(solution)/shard_map/ppermute | solution.py:197
  124.6 47.4 %collective-permute-start.5 = (f32[3,256,256]{2,1,0:T(8,128)S(1)}, f32[3,256,256]{2,1,0:T(8,128)}, u32[]{:S(2)}, u32[]{:S(2)}) collective-permute-start(f32[3,256,256]{2,1,0:T(8,128)S(1)} %get-tuple-element.13), channel_id=1, source_target_pairs={{0,9},{1,10},{2,11},{3,12},{4,13},{5,14},{6,15},{8,17},{9,18},{10,... | collective-permute-start | bytes 2359304 | tf_op jit(solution)/shard_map/ppermute | solution.py:197
  174.5 17.2 %collective-permute-start.8 = (f32[2,256]{1,0:T(2,128)S(1)}, f32[2,256]{1,0:T(2,128)S(1)}, u32[]{:S(2)}, u32[]{:S(2)}) collective-permute-start(f32[2,256]{1,0:T(2,128)S(1)} %get-tuple-element.9), channel_id=1, source_target_pairs={{1,0},{2,1},{3,2},{4,3},{5,4},{6,5},{7,6},{9,8},{10,9},{11,10},{12... | collective-permute-start | bytes 6152 | tf_op jit(solution)/shard_map/ppermute | solution.py:197
  176.4 15.4 %collective-permute-start.9 = (f32[2,256]{1,0:T(2,128)S(1)}, f32[2,256]{1,0:T(2,128)S(1)}, u32[]{:S(2)}, u32[]{:S(2)}) collective-permute-start(f32[2,256]{1,0:T(2,128)S(1)} %get-tuple-element.8), channel_id=1, source_target_pairs={{0,1},{1,2},{2,3},{3,4},{4,5},{5,6},{6,7},{8,9},{9,10},{10,11},{11... | collective-permute-start | bytes 6152 | tf_op jit(solution)/shard_map/ppermute | solution.py:197
  179.8 12.2 %collective-permute-start.6 = (f32[2,256]{1,0:T(2,128)S(1)}, f32[2,256]{1,0:T(2,128)S(1)}, u32[]{:S(2)}, u32[]{:S(2)}) collective-permute-start(f32[2,256]{1,0:T(2,128)S(1)} %bitcast.18), channel_id=1, source_target_pairs={{8,0},{9,1},{10,2},{11,3},{12,4},{13,5},{14,6},{15,7},{16,8},{17,9... | collective-permute-start | bytes 6152 | tf_op jit(solution)/shard_map/ppermute | solution.py:197
  190.1 3.1 %collective-permute-start.7 = (f32[2,256]{1,0:T(2,128)S(1)}, f32[2,256]{1,0:T(2,128)S(1)}, u32[]{:S(2)}, u32[]{:S(2)}) collective-permute-start(f32[2,256]{1,0:T(2,128)S(1)} %bitcast.19), channel_id=1, source_target_pairs={{0,8},{1,9},{2,10},{3,11},{4,12},{5,13},{6,14},{7,15},{8,16},{9,17... | collective-permute-start | bytes 6152 | tf_op jit(solution)/shard_map/ppermute | solution.py:197
Sparse Core Ops, SparseCore 0:
  126.1 160.5 all-reduce.2

commit v2 on v1

--- a/solution.py
+++ b/solution.py
@@ -34,7 +34,11 @@
     tw = np.stack([np.cos(turn), np.sin(turn)]).astype(np.float32)
     rows = np.broadcast_to(tw[:, None, :], (2, 8, half)).copy()
     cols = np.broadcast_to(tw[:, :, None], (2, half, frame)).copy()
-    return right_f, right_i, left_f, left_i, rows, cols
+    order = np.arange(frame)
+    order = np.where(order < half, 2 * order, 2 * (order - half) + 1)
+    move = np.eye(frame)[order].astype(ml_dtypes.bfloat16)
+    moves = np.concatenate([move, move, move], axis=1)
+    return right_f, right_i, left_f, left_i, rows, cols, moves, moves.T.copy()
 
 
 def split(x):
@@ -42,6 +46,12 @@
     return high, (x - high.astype(F32)).astype(BF16)
 
 
+def split_exact(x):
+    high = x.astype(BF16)
+    rest = x - high.astype(F32)
+    return (high,) + split(rest)
+
+
 def right_dot(x, table):
     high, low = split(x)
     return jnp.dot(jnp.concatenate([high, low, high], axis=1), table, preferred_element_type=F32)
@@ -53,14 +63,25 @@
 
 
 def waves_kernel(
-    place, live, own, right, down, diag, probe, amplitude, rf, ri, lf, li, twr, twc,
-    totals, grad, power, spectra, ratio, accum,
+    place, live, own, right, down, diag, probe, amplitude, rf, ri, lf, li, twr, twc, rows_to, cols_to,
+    totals, grad, spectra, ratio, accum,
 ):
     modes, frame = probe.shape[1], probe.shape[2]
     half = frame // 2
     slots = amplitude.shape[0]
     tile = own.shape[1]
     cat = jnp.concatenate
+
+    def put(plane, value, first):
+        blocks = frame // 8
+        for part in range(frame // 128):
+            where = pl.ds((plane * (frame // 128) + part) * blocks, blocks)
+            piece = value[:, part * 128 : (part + 1) * 128].reshape(blocks, 8, 128)
+            grad[where] = piece if first else grad[where] + piece
+
+    used = (2 * modes + 1) * (frame // 128) * (frame // 8)
+    if grad.shape[0] > used:
+        grad[used:] = jnp.zeros((grad.shape[0] - used, 8, 128), F32)
 
     for slot in range(slots):
         row, col = place[0, slot], place[1, slot]
@@ -112,7 +133,13 @@
                 axis=0,
             )
 
-        scale = amplitude[slot] * lax.rsqrt(jnp.maximum(accum[2], INTENSITY_FLOOR))
+        sorted_cols = jnp.dot(
+            cat(split_exact(amplitude[slot]), axis=1), cols_to[...], preferred_element_type=F32
+        )
+        sorted_all = jnp.dot(
+            rows_to[...], cat(split_exact(sorted_cols), axis=0), preferred_element_type=F32
+        )
+        scale = sorted_all * lax.rsqrt(jnp.maximum(accum[2], INTENSITY_FLOOR))
         ratio[:half, :frame] = scale[:half]
         ratio[half:, :frame] = scale[:half]
         ratio[:half, frame:] = scale[half:]
@@ -143,14 +170,11 @@
             accum[3] += pr * bi - pi * br
             accum[4] += flag * (pr * pr + pi * pi)
             gr, gi = qr * br + qi * bi, qr * bi - qi * br
-            if slot == 0:
-                grad[0, m], grad[1, m] = gr, gi
-            else:
-                grad[0, m] += gr
-                grad[1, m] += gi
+            put(m, gr, slot == 0)
+            put(modes + m, gi, slot == 0)
 
         strength = flag * (qr * qr + qi * qi)
-        power[...] = strength if slot == 0 else power[...] + strength
+        put(2 * modes, strength, slot == 0)
         for part in range(3):
             piece = accum[2 + part]
             piece = cat([piece, jnp.zeros((frame, width - frame), F32)], axis=1)
@@ -160,7 +184,7 @@
             totals[part] = piece if slot == 0 else totals[part] + piece
 
 
-def waves(place, live, own, right, down, diag, probe, amplitude):
+def waves(place, live, own, right, down, diag, probe, amplitude, chunks):
     modes, frame = probe.shape[1], probe.shape[2]
     tile = own.shape[1]
     smem = pl.BlockSpec(memory_space=pltpu.SMEM)
@@ -169,11 +193,10 @@
         waves_kernel,
         out_shape=(
             jax.ShapeDtypeStruct((3, 2 * tile, 2 * tile), F32),
-            jax.ShapeDtypeStruct(probe.shape, F32),
-            jax.ShapeDtypeStruct((frame, frame), F32),
+            jax.ShapeDtypeStruct((chunks, 8, 128), F32),
         ),
-        in_specs=[smem] * 2 + [vmem] * 12,
-        out_specs=(vmem, vmem, vmem),
+        in_specs=[smem] * 2 + [vmem] * 14,
+        out_specs=(vmem, vmem),
         scratch_shapes=[
             pltpu.VMEM((modes, frame, 2 * frame), F32),
             pltpu.VMEM((frame, 2 * frame), F32),
@@ -197,6 +220,235 @@
     return lax.ppermute(value, ("row", "col"), pairs)
 
 
+def exchange_kernel(
+    rows, cols, parts, grad, totals, own, probe, new_object, new_probe,
+    acc, inbox, full, quads, upd, row_edges, col_edges, inverse,
+    send_sem, recv_sem, quad_send, quad_recv, edge_send, edge_recv,
+):
+    r, c = lax.axis_index("row"), lax.axis_index("col")
+    tile = own.shape[1]
+    modes, frame = probe.shape[1], probe.shape[2]
+    row_bits, col_bits = rows.bit_length() - 1, cols.bit_length() - 1
+    core = [(0, bit) for bit in range(row_bits)][:1]
+    far = [(0, bit) for bit in range(row_bits)][1:]
+    low = [(1, bit) for bit in range(col_bits // 2)]
+    high = [(1, bit) for bit in range(col_bits // 2, col_bits)]
+    orders = [core + far + low + high, core + low + high + far, core + high + far + low]
+    stages = row_bits + col_bits
+
+    def partner(axis, bit):
+        step = 1 << bit
+        mine = (c if axis else r) // step % 2
+        shift = step - 2 * step * mine
+        return mine, ((r, c + shift) if axis else (r + shift, c))
+
+    def near(dr, dc):
+        good = jnp.bool_(True)
+        if dr > 0:
+            good = jnp.logical_and(good, r < rows - dr)
+        if dr < 0:
+            good = jnp.logical_and(good, r >= -dr)
+        if dc > 0:
+            good = jnp.logical_and(good, c < cols - dc)
+        if dc < 0:
+            good = jnp.logical_and(good, c >= -dc)
+        return good, (r + dr, c + dc)
+
+    row_edges[...] = jnp.zeros_like(row_edges)
+    col_edges[...] = jnp.zeros_like(col_edges)
+    barrier = pltpu.get_barrier_semaphore()
+    for axis, bit in orders[0]:
+        pl.semaphore_signal(
+            barrier, inc=1, device_id=partner(axis, bit)[1], device_id_type=pl.DeviceIdType.MESH
+        )
+    expected = jnp.int32(stages)
+    for dr, dc in ((0, 1), (1, 0), (1, 1), (0, -1), (-1, 0), (-1, -1)):
+        good, there = near(dr, dc)
+
+        @pl.when(good)
+        def _():
+            pl.semaphore_signal(
+                barrier, inc=1, device_id=there, device_id_type=pl.DeviceIdType.MESH
+            )
+
+        expected = expected + jnp.where(good, 1, 0)
+    pl.semaphore_wait(barrier, expected)
+
+    def remote(source, target, send, recv, there):
+        return pltpu.make_async_remote_copy(
+            src_ref=source, dst_ref=target, send_sem=send, recv_sem=recv,
+            device_id=there, device_id_type=pl.DeviceIdType.MESH,
+        )
+
+    ranges = [[start] for start in parts]
+    slots = [0]
+    copies = {}
+
+    def halve(p, stage):
+        start, size = ranges[p][stage]
+        mine, there = partner(*orders[p][stage])
+        half = size // 2
+        box = pl.ds(slots[0], half)
+        slots[0] += half
+        source = (grad if stage == 0 else acc).at[pl.ds(start + (1 - mine) * half, half)]
+        copy = remote(
+            source, inbox.at[box], send_sem.at[0, p, stage], recv_sem.at[0, p, stage], there
+        )
+        copy.start()
+        ranges[p].append((start + mine * half, half))
+        copies[p, stage] = (copy, box)
+
+    def add(p, stage):
+        copy, box = copies[p, stage]
+        copy.wait()
+        keep = pl.ds(*ranges[p][stage + 1])
+        target = full if stage + 1 == stages else acc
+        target[keep] = (grad if stage == 0 else acc)[keep] + inbox[box]
+
+    def spread(p, stage):
+        there = partner(*orders[p][stage])[1]
+        keep = pl.ds(*ranges[p][stage + 1])
+        copy = remote(
+            full.at[keep], full.at[keep], send_sem.at[1, p, stage], recv_sem.at[1, p, stage], there
+        )
+        copy.start()
+        copies[p, stage] = (copy, None)
+
+    every = range(len(parts))
+    for p in every:
+        halve(p, 0)
+    sides = ((0, 1), (1, 0), (1, 1))
+    quadrants = []
+    for k, (dr, dc) in enumerate(sides):
+        source = totals.at[:, pl.ds(dr * tile, tile), pl.ds(dc * tile, tile)]
+        good, there = near(dr, dc)
+        copy = remote(source, quads.at[k], quad_send.at[k], quad_recv.at[k], there)
+        pl.when(good)(copy.start)
+        quadrants.append((good, near(-dr, -dc)[0], copy))
+    for stage in range(stages):
+        for p in every:
+            add(p, stage)
+            if stage + 1 < stages:
+                halve(p, stage + 1)
+            else:
+                spread(p, stage)
+
+    def update():
+        upd[...] = totals[:, :tile, :tile]
+        for k, (good, gets, copy) in enumerate(quadrants):
+            pl.when(good)(copy.wait_send)
+
+            @pl.when(gets)
+            def _():
+                copy.wait_recv()
+                upd[...] += quads[k]
+
+        below = upd[2] + OBJECT_DELTA
+        upd[0] = own[0] + upd[0] / below
+        upd[1] = own[1] + upd[1] / below
+        borders = (
+            ((1, 0), upd.at[:2, pl.ds(tile - 8, 8)], row_edges.at[0]),
+            ((-1, 0), upd.at[:2, pl.ds(0, 8)], row_edges.at[1]),
+            ((0, 1), upd.at[:2, :, pl.ds(tile - 128, 128)], col_edges.at[0]),
+            ((0, -1), upd.at[:2, :, pl.ds(0, 128)], col_edges.at[1]),
+        )
+        edges = []
+        for k, ((dr, dc), source, target) in enumerate(borders):
+            good, there = near(dr, dc)
+            copy = remote(source, target, edge_send.at[k], edge_recv.at[k], there)
+            pl.when(good)(copy.start)
+            edges.append((good, near(-dr, -dc)[0], copy))
+        return edges
+
+    def smooth(edges):
+        for good, gets, copy in edges:
+            pl.when(good)(copy.wait_send)
+            pl.when(gets)(copy.wait_recv)
+        for part in range(2):
+            value = upd[part]
+            above, below = row_edges[0, part, 7:8], row_edges[1, part, 0:1]
+            before, after = col_edges[0, part][:, 127:128], col_edges[1, part][:, 0:1]
+            neighbours = (
+                jnp.concatenate([value[1:], below], axis=0)
+                + jnp.concatenate([above, value[:-1]], axis=0)
+                + jnp.concatenate([value[:, 1:], after], axis=1)
+                + jnp.concatenate([before, value[:, :-1]], axis=1)
+            )
+            new_object[part] = value + SMOOTH_WEIGHT * (neighbours - 4.0 * value)
+
+    update_at, smooth_at = min(2, stages - 1), min(1, stages - 1)
+    edges = None
+    for stage in reversed(range(stages)):
+        for p in every:
+            copies[p, stage][0].wait()
+            if stage > 0:
+                spread(p, stage - 1)
+        if stage == update_at:
+            edges = update()
+        if stage == smooth_at:
+            smooth(edges)
+
+    blocks = frame // 8
+    for part in range(frame // 128):
+        lanes = pl.ds(part * 128, 128)
+
+        def plane(index):
+            where = pl.ds((index * (frame // 128) + part) * blocks, blocks)
+            return full[where].reshape(frame, 128)
+
+        inverse[...] = 1.0 / (plane(2 * modes) + PROBE_DELTA)
+
+        @pl.loop(0, modes)
+        def _(m):
+            new_probe[0, m, :, lanes] = probe[0, m, :, lanes] + plane(m) * inverse[...]
+            new_probe[1, m, :, lanes] = probe[1, m, :, lanes] + plane(modes + m) * inverse[...]
+
+
+def cut(probe, devices):
+    modes, frame = probe.shape[1], probe.shape[2]
+    used = (2 * modes + 1) * (frame // 128) * (frame // 8)
+    units = -(-used // devices)
+    bounds = [units * k // 3 * devices for k in range(4)]
+    return units * devices, [(a, b - a) for a, b in zip(bounds, bounds[1:]) if b > a]
+
+
+def exchange(grad, totals, own, probe, parts):
+    rows, cols = lax.axis_size("row"), lax.axis_size("col")
+    frame, tile = probe.shape[2], own.shape[1]
+    stages = (rows * cols).bit_length() - 1
+    vmem = pl.BlockSpec(memory_space=pltpu.VMEM)
+    dma = pltpu.SemaphoreType.DMA
+    return pl.pallas_call(
+        functools.partial(exchange_kernel, rows, cols, parts),
+        out_shape=(
+            jax.ShapeDtypeStruct(own.shape, F32),
+            jax.ShapeDtypeStruct(probe.shape, F32),
+        ),
+        in_specs=[vmem] * 4,
+        out_specs=(vmem, vmem),
+        scratch_shapes=[
+            pltpu.VMEM(grad.shape, F32),
+            pltpu.VMEM(grad.shape, F32),
+            pltpu.VMEM(grad.shape, F32),
+            pltpu.VMEM((3, 3, tile, tile), F32),
+            pltpu.VMEM((3, tile, tile), F32),
+            pltpu.VMEM((2, 2, 8, tile), F32),
+            pltpu.VMEM((2, 2, tile, 128), F32),
+            pltpu.VMEM((frame, 128), F32),
+            dma((2, len(parts), stages)),
+            dma((2, len(parts), stages)),
+            dma((3,)),
+            dma((3,)),
+            dma((4,)),
+            dma((4,)),
+        ],
+        compiler_params=pltpu.CompilerParams(
+            vmem_limit_bytes=48 << 20, collective_id=0, has_side_effects=True
+        ),
+        cost_estimate=pl.CostEstimate(flops=1 << 22, bytes_accessed=24 << 20, transcendentals=0),
+    )(grad, totals, own, probe)
+
+
 def per_device(object_field, probe_modes, patterns, offsets, counts):
     tile, frame = object_field.shape[1], probe_modes.shape[-1]
     slots = patterns.shape[0]
@@ -206,29 +458,11 @@
     base = jnp.stack([lax.axis_index("row"), lax.axis_index("col")]).astype(jnp.int32) * tile
     place = offsets - base[:, None]
     live = (jnp.arange(slots, dtype=jnp.int32) < counts[0]).astype(jnp.int32)
-    half = frame // 2
-    amplitude = patterns.reshape(slots, half, 2, half, 2).transpose(0, 2, 1, 4, 3)
-    amplitude = amplitude.reshape(slots, frame, frame)
-    totals, gradient, power = waves(
-        place, live, object_field, right, down, diag, probe_modes, amplitude
+    chunks, parts = cut(probe_modes, lax.axis_size("row") * lax.axis_size("col"))
+    totals, gradient = waves(
+        place, live, object_field, right, down, diag, probe_modes, patterns, chunks
     )
-    gradient_all, power_all = lax.psum((gradient, power), ("row", "col"))
-    sums = totals[:, :tile, :tile] + moved(totals[:, :tile, tile:], 0, 1)
-    sums = sums + moved(totals[:, tile:, :tile], 1, 0) + moved(totals[:, tile:, tile:], 1, 1)
-    updated = object_field + sums[:2] / (sums[2] + OBJECT_DELTA)
-    above = moved(updated[:, -1, :], 1, 0)
-    below = moved(updated[:, 0, :], -1, 0)
-    before = moved(updated[:, :, -1], 0, 1)
-    after = moved(updated[:, :, 0], 0, -1)
-    neighbours = (
-        jnp.concatenate([updated[:, 1:], below[:, None]], axis=1)
-        + jnp.concatenate([above[:, None], updated[:, :-1]], axis=1)
-        + jnp.concatenate([updated[:, :, 1:], after[:, :, None]], axis=2)
-        + jnp.concatenate([before[:, :, None], updated[:, :, :-1]], axis=2)
-    )
-    new_object = updated + SMOOTH_WEIGHT * (neighbours - 4.0 * updated)
-    new_probe = probe_modes + gradient_all / (power_all[None, None] + PROBE_DELTA)
-    return (new_object, new_probe)
+    return exchange(gradient, totals, object_field, probe_modes, parts)
 
 
 def solution(mesh):

time: 305 us -> 199 us (0.65)
  the two profiles are of different devices: /device:TPU:13 before, /device:TPU:28 now
where the time goes in v2:
time: 199 us; the launch traced here: 198 us
  Pallas kernels  153 us (77%)
  waiting for transfers between devices  18.1 us (9%)
  local copies, waits for them, and re-layouts  17 us (9%)
  starting transfers between devices  7.87 us (4%)
    pallas_call x1, Pallas kernels, exchange(): pl.pallas_call(functools.partial(exchange_kernel, rows, cols, parts), out...  106 us
    pallas_call x1, Pallas kernels, waves(): pl.pallas_call(waves_kernel, out_shape=(jax.ShapeDtypeStruct((3, 2 * tile...  46.8 us
    ppermute x3, waiting for transfers between devices, moved(): return lax.ppermute(value, ('row', 'col'), pairs)  18.1 us
    unnamed x26, local copies, waits for them, and re-layouts  17 us
    ppermute x3, starting transfers between devices, moved(): return lax.ppermute(value, ('row', 'col'), pairs)  7.87 us
  transfers between devices with their start and end apart: 3, of which 3 were waited for; matrix products, arithmetic and copies ran while one was open for 0% of the time, Pallas kernels for 0%

profile of v2, /device:TPU:28, one launch (start us, length us, event | category | flops | bytes accessed | tf_op | source)
XLA Modules:
  0.0 198.2 jit_solution(16478362638549449534)
XLA Ops:
  0.6 2.7 %collective-permute-start.2 = (f32[2,256,256]{2,1,0:T(8,128)}, f32[2,256,256]{2,1,0:T(8,128)S(1)}, u32[]{:S(2)}, u32[]{:S(2)}) collective-permute-start(f32[2,256,256]{2,1,0:T(8,128)} %own.3), channel_id=1, source_target_pairs={{9,0},{10,1},{11,2},{12,3},{13,4},{14,5},{15,6},{17,8},{18,9},{19,... | collective-permute-start | bytes 1572872 | tf_op jit(solution)/shard_map/ppermute | solution.py:220
  3.3 2.8 %collective-permute-start.1 = (f32[2,256,256]{2,1,0:T(8,128)}, f32[2,256,256]{2,1,0:T(8,128)S(1)}, u32[]{:S(2)}, u32[]{:S(2)}) collective-permute-start(f32[2,256,256]{2,1,0:T(8,128)} %own.3), channel_id=1, source_target_pairs={{8,0},{9,1},{10,2},{11,3},{12,4},{13,5},{14,6},{15,7},{16,8},{17,9... | collective-permute-start | bytes 1572872 | tf_op jit(solution)/shard_map/ppermute | solution.py:220
  6.1 2.4 %collective-permute-start = (f32[2,256,256]{2,1,0:T(8,128)}, f32[2,256,256]{2,1,0:T(8,128)S(1)}, u32[]{:S(2)}, u32[]{:S(2)}) collective-permute-start(f32[2,256,256]{2,1,0:T(8,128)} %own.3), channel_id=1, source_target_pairs={{1,0},{2,1},{3,2},{4,3},{5,4},{6,5},{7,6},{9,8},{10,9},{11,10},{12... | collective-permute-start | bytes 1572872 | tf_op jit(solution)/shard_map/ppermute | solution.py:220
  9.2 0.1 add_multiply_fusion
  9.3 0.7 broadcast_subtract_fusion.place
  10.0 6.9 %collective-permute-done.2.diag = f32[2,256,256]{2,1,0:T(8,128)S(1)} collective-permute-done((f32[2,256,256]{2,1,0:T(8,128)}, f32[2,256,256]{2,1,0:T(8,128)S(1)}, u32[]{:S(2)}, u32[]{:S(2)}) %collective-permute-start.2) | collective-permute-done | bytes 524320 | tf_op jit(solution)/shard_map/ppermute | solution.py:220
  17.0 0.4 collective-permute-done.1.down
  17.3 10.8 %collective-permute-done.right = f32[2,256,256]{2,1,0:T(8,128)S(1)} collective-permute-done((f32[2,256,256]{2,1,0:T(8,128)}, f32[2,256,256]{2,1,0:T(8,128)S(1)}, u32[]{:S(2)}, u32[]{:S(2)}) %collective-permute-start) | collective-permute-done | bytes 524320 | tf_op jit(solution)/shard_map/ppermute | solution.py:220
  28.1 0.0 copy-start.1
  28.1 1.0 copy-done.1
  29.2 0.0 copy-start.3
  29.2 1.0 copy-done.3
  30.2 0.0 copy-start.4
  30.2 1.0 copy-done.4
  31.2 0.0 copy-start.5
  31.2 1.0 copy-done.5
  32.2 0.0 copy-start.6
  32.2 1.0 copy-done.6
  33.2 0.0 copy-start.7
  33.2 1.0 copy-done.7
  34.2 0.0 copy-start.8
  34.2 1.0 copy-done.8
  35.2 0.0 copy-start.9
  35.2 1.0 copy-done.9
  36.2 0.0 copy-start.10
  36.2 0.9 copy-done.10
  37.1 0.0 copy-start.11
  37.1 0.7 copy-done.11
  37.8 0.0 copy-start.2
  37.8 46.8 %shard_map.140 = (f32[3,512,512]{2,1,0:T(8,128)}, f32[1088,8,128]{2,1,0:T(8,128)}) custom-call(s32[2,2]{1,0:T(2,128)S(1)} %broadcast_subtract_fusion.place, s32[2]{0:T(128)S(1)} %compare_convert_fusion.live, f32[2,256,256]{2,1,0:T(8,128)S(1)} %copy-done.1, f32[2,256,256]{2,1,0:T(8,128)S(1)} %collective-permute-done.right, ...), custom_call_target="tpu_custom_call" | custom-call | flops 60000002048 | bytes 16777216 | tf_op jit(solution)/shard_map/pallas_call | solution.py:192
  84.6 0.0 copy-done.2
  84.6 0.0 copy-start
  84.6 1.9 copy-done
  86.5 106.3 %shard_map.141 = (f32[2,256,256]{2,1,0:T(8,128)S(1)}, f32[2,8,256,256]{3,2,1,0:T(8,128)}) custom-call(f32[1088,8,128]{2,1,0:T(8,128)} %get-tuple-element.4.grad, f32[3,512,512]{2,1,0:T(8,128)S(1)} %copy-done, f32[2,256,256]{2,1,0:T(8,128)S(1)} %copy-done.2, f32[2,8,256,256]{3,2,1,0:T(8,128)} %probe.3), custom_call_target="tpu_custom_call" | custom-call | flops 4194304 | bytes 25165824 | tf_op jit(solution)/shard_map/pallas_call | solution.py:421
  192.8 0.8 copy.18
  193.6 4.6 %copy.19 = f32[2,8,256,256]{3,2,1,0:T(8,128)} copy(f32[2,8,256,256]{3,2,1,0:T(8,128)} %get-tuple-element.9) | data formatting | bytes 8388608
  (1 shorter events, 0.0 us)
Async XLA Ops:
  0.6 16.3 %collective-permute-start.2 = (f32[2,256,256]{2,1,0:T(8,128)}, f32[2,256,256]{2,1,0:T(8,128)S(1)}, u32[]{:S(2)}, u32[]{:S(2)}) collective-permute-start(f32[2,256,256]{2,1,0:T(8,128)} %own.3), channel_id=1, source_target_pairs={{9,0},{10,1},{11,2},{12,3},{13,4},{14,5},{15,6},{17,8},{18,9},{19,... | collective-permute-start | bytes 1572872 | tf_op jit(solution)/shard_map/ppermute | solution.py:220
  3.3 14.0 %collective-permute-start.1 = (f32[2,256,256]{2,1,0:T(8,128)}, f32[2,256,256]{2,1,0:T(8,128)S(1)}, u32[]{:S(2)}, u32[]{:S(2)}) collective-permute-start(f32[2,256,256]{2,1,0:T(8,128)} %own.3), channel_id=1, source_target_pairs={{8,0},{9,1},{10,2},{11,3},{12,4},{13,5},{14,6},{15,7},{16,8},{17,9... | collective-permute-start | bytes 1572872 | tf_op jit(solution)/shard_map/ppermute | solution.py:220
  6.1 22.0 %collective-permute-start = (f32[2,256,256]{2,1,0:T(8,128)}, f32[2,256,256]{2,1,0:T(8,128)S(1)}, u32[]{:S(2)}, u32[]{:S(2)}) collective-permute-start(f32[2,256,256]{2,1,0:T(8,128)} %own.3), channel_id=1, source_target_pairs={{1,0},{2,1},{3,2},{4,3},{5,4},{6,5},{7,6},{9,8},{10,9},{11,10},{12... | collective-permute-start | bytes 1572872 | tf_op jit(solution)/shard_map/ppermute | solution.py:220
  28.1 1.0 copy-start.1
  29.2 1.0 copy-start.3
  30.2 1.0 copy-start.4
  31.2 1.0 copy-start.5
  32.2 1.0 copy-start.6
  33.2 1.0 copy-start.7
  34.2 1.0 copy-start.8
  35.2 1.0 copy-start.9
  36.2 0.9 copy-start.10
  37.1 0.7 copy-start.11
  37.8 46.8 %copy-start.2 = (f32[2,256,256]{2,1,0:T(8,128)S(1)}, f32[2,256,256]{2,1,0:T(8,128)}, u32[]{:S(2)}) copy-start(f32[2,256,256]{2,1,0:T(8,128)} %own.3) | copy-start | bytes 1572868
  84.6 1.9 copy-start

commit v3 on v2

--- a/solution.py
+++ b/solution.py
@@ -16,6 +16,7 @@
 SMOOTH_WEIGHT = 0.1
 F32 = jnp.float32
 BF16 = jnp.bfloat16
+UNROLL = 1
 
 
 def tables(frame):
@@ -26,19 +27,15 @@
     full = np.block([[c, s], [-s, c]]).astype(np.float32)
     high = full.astype(ml_dtypes.bfloat16)
     low = (full - high.astype(np.float32)).astype(ml_dtypes.bfloat16)
-    right_f = np.concatenate([high, high, low], axis=0)
-    right_i = np.concatenate([high.T, high.T, low.T], axis=0)
-    left_f = np.concatenate([high.T, high.T, low.T], axis=1)
-    left_i = np.concatenate([high, high, low], axis=1)
     turn = -2.0 * np.pi * n / frame
     tw = np.stack([np.cos(turn), np.sin(turn)]).astype(np.float32)
-    rows = np.broadcast_to(tw[:, None, :], (2, 8, half)).copy()
-    cols = np.broadcast_to(tw[:, :, None], (2, half, frame)).copy()
+    rows = np.zeros((2, 8, frame), np.float32)
+    rows[:, :, :half] = tw[:, None, :]
+    cols = np.broadcast_to(tw[:, :, None], (2, half, frame))
     order = np.arange(frame)
     order = np.where(order < half, 2 * order, 2 * (order - half) + 1)
     move = np.eye(frame)[order].astype(ml_dtypes.bfloat16)
-    moves = np.concatenate([move, move, move], axis=1)
-    return right_f, right_i, left_f, left_i, rows, cols, moves, moves.T.copy()
+    return np.stack([high, low, high.T, low.T, move, move.T]), np.concatenate([cols, rows], axis=1)
 
 
 def split(x):
@@ -63,7 +60,7 @@
 
 
 def waves_kernel(
-    place, live, own, right, down, diag, probe, amplitude, rf, ri, lf, li, twr, twc, rows_to, cols_to,
+    place, live, own, right, down, diag, probe, amplitude, matrices, turns,
     totals, grad, spectra, ratio, accum,
 ):
     modes, frame = probe.shape[1], probe.shape[2]
@@ -71,6 +68,9 @@
     slots = amplitude.shape[0]
     tile = own.shape[1]
     cat = jnp.concatenate
+
+    def stacked(high, low, axis):
+        return cat([matrices[high], matrices[high], matrices[low]], axis=axis)
 
     def put(plane, value, first):
         blocks = frame // 8
@@ -98,11 +98,11 @@
         accum[0], accum[1] = qr, qi
         accum[2] = jnp.zeros((frame, frame), F32)
 
-        @pl.loop(0, modes)
+        @pl.loop(0, modes, unroll=UNROLL)
         def _(m):
             qr, qi, pr, pi = accum[0], accum[1], probe[0, m], probe[1, m]
             wr, wi = pr * qr - pi * qi, pr * qi + pi * qr
-            c, s = twr[0, 0:1], twr[1, 0:1]
+            c, s = turns[0, half : half + 1, :half], turns[1, half : half + 1, :half]
             dr, di = wr[:, :half] - wr[:, half:], wi[:, :half] - wi[:, half:]
             x = cat(
                 [
@@ -111,10 +111,10 @@
                 ],
                 axis=0,
             )
-            y = right_dot(x, rf[...])
+            y = right_dot(x, stacked(0, 1, 0))
             yr = cat([y[:frame, :half], y[frame:, :half]], axis=1)
             yi = cat([y[:frame, half:], y[frame:, half:]], axis=1)
-            c, s = twc[0], twc[1]
+            c, s = turns[0, :half], turns[1, :half]
             dr, di = yr[:half] - yr[half:], yi[:half] - yi[half:]
             z = cat(
                 [
@@ -123,7 +123,7 @@
                 ],
                 axis=1,
             )
-            r = left_dot(lf[...], z)
+            r = left_dot(stacked(2, 3, 1), z)
             spectra[m] = r
             accum[2] += cat(
                 [
@@ -134,10 +134,10 @@
             )
 
         sorted_cols = jnp.dot(
-            cat(split_exact(amplitude[slot]), axis=1), cols_to[...], preferred_element_type=F32
+            cat(split_exact(amplitude[slot]), axis=1), stacked(5, 5, 0), preferred_element_type=F32
         )
         sorted_all = jnp.dot(
-            rows_to[...], cat(split_exact(sorted_cols), axis=0), preferred_element_type=F32
+            stacked(4, 4, 1), cat(split_exact(sorted_cols), axis=0), preferred_element_type=F32
         )
         scale = sorted_all * lax.rsqrt(jnp.maximum(accum[2], INTENSITY_FLOOR))
         ratio[:half, :frame] = scale[:half]
@@ -147,10 +147,10 @@
         for part in range(3):
             accum[2 + part] = jnp.zeros((frame, frame), F32)
 
-        @pl.loop(0, modes)
+        @pl.loop(0, modes, unroll=UNROLL)
         def _(m):
-            r = left_dot(li[...], spectra[m] * ratio[...])
-            c, s = twc[0], twc[1]
+            r = left_dot(stacked(0, 1, 1), spectra[m] * ratio[...])
+            c, s = turns[0, :half], turns[1, :half]
             er, ei, dr, di = r[:half, :frame], r[half:, :frame], r[:half, frame:], r[half:, frame:]
             vr, vi = dr * c + di * s, di * c - dr * s
             yr = cat([er + vr, er - vr], axis=0)
@@ -159,8 +159,8 @@
                 [cat([yr[:, :half], yi[:, :half]], axis=1), cat([yr[:, half:], yi[:, half:]], axis=1)],
                 axis=0,
             )
-            y = right_dot(x, ri[...])
-            c, s = twr[0, 0:1], twr[1, 0:1]
+            y = right_dot(x, stacked(2, 3, 0))
+            c, s = turns[0, half : half + 1, :half], turns[1, half : half + 1, :half]
             er, ei, dr, di = y[:frame, :half], y[:frame, half:], y[frame:, :half], y[frame:, half:]
             vr, vi = dr * c + di * s, di * c - dr * s
             qr, qi, pr, pi = accum[0], accum[1], probe[0, m], probe[1, m]
@@ -195,7 +195,7 @@
             jax.ShapeDtypeStruct((3, 2 * tile, 2 * tile), F32),
             jax.ShapeDtypeStruct((chunks, 8, 128), F32),
         ),
-        in_specs=[smem] * 2 + [vmem] * 14,
+        in_specs=[smem] * 2 + [vmem] * 8,
         out_specs=(vmem, vmem),
         scratch_shapes=[
             pltpu.VMEM((modes, frame, 2 * frame), F32),
@@ -222,7 +222,7 @@
 
 def exchange_kernel(
     rows, cols, parts, grad, totals, own, probe, new_object, new_probe,
-    acc, inbox, full, quads, upd, row_edges, col_edges, inverse,
+    acc, inbox, full, fallen, wide, pushed, upd, row_edges, col_edges, inverse,
     send_sem, recv_sem, quad_send, quad_recv, edge_send, edge_recv,
 ):
     r, c = lax.axis_index("row"), lax.axis_index("col")
@@ -262,7 +262,7 @@
             barrier, inc=1, device_id=partner(axis, bit)[1], device_id_type=pl.DeviceIdType.MESH
         )
     expected = jnp.int32(stages)
-    for dr, dc in ((0, 1), (1, 0), (1, 1), (0, -1), (-1, 0), (-1, -1)):
+    for dr, dc in ((0, 1), (1, 0), (0, -1), (-1, 0)):
         good, there = near(dr, dc)
 
         @pl.when(good)
@@ -317,14 +317,31 @@
     every = range(len(parts))
     for p in every:
         halve(p, 0)
-    sides = ((0, 1), (1, 0), (1, 1))
-    quadrants = []
-    for k, (dr, dc) in enumerate(sides):
-        source = totals.at[:, pl.ds(dr * tile, tile), pl.ds(dc * tile, tile)]
-        good, there = near(dr, dc)
-        copy = remote(source, quads.at[k], quad_send.at[k], quad_recv.at[k], there)
+    def send_down():
+        good, there = near(1, 0)
+        copy = remote(
+            totals.at[:, pl.ds(tile, tile)], fallen, quad_send.at[0], quad_recv.at[0], there
+        )
         pl.when(good)(copy.start)
-        quadrants.append((good, near(-dr, -dc)[0], copy))
+        return good, near(-1, 0)[0], copy
+
+    def send_right(good, gets, copy):
+        wide[...] = totals[:, :tile]
+        pl.when(good)(copy.wait_send)
+
+        @pl.when(gets)
+        def _():
+            copy.wait_recv()
+            wide[...] += fallen[...]
+
+        good, there = near(0, 1)
+        copy = remote(
+            wide.at[:, :, pl.ds(tile, tile)], pushed, quad_send.at[1], quad_recv.at[1], there
+        )
+        pl.when(good)(copy.start)
+        return good, near(0, -1)[0], copy
+
+    sideways = send_down()
     for stage in range(stages):
         for p in every:
             add(p, stage)
@@ -332,16 +349,18 @@
                 halve(p, stage + 1)
             else:
                 spread(p, stage)
+        if stage == min(1, stages - 1):
+            sideways = send_right(*sideways)
 
     def update():
-        upd[...] = totals[:, :tile, :tile]
-        for k, (good, gets, copy) in enumerate(quadrants):
-            pl.when(good)(copy.wait_send)
-
-            @pl.when(gets)
-            def _():
-                copy.wait_recv()
-                upd[...] += quads[k]
+        good, gets, copy = sideways
+        upd[...] = wide[:, :, :tile]
+        pl.when(good)(copy.wait_send)
+
+        @pl.when(gets)
+        def _():
+            copy.wait_recv()
+            upd[...] += pushed[...]
 
         below = upd[2] + OBJECT_DELTA
         upd[0] = own[0] + upd[0] / below
@@ -430,15 +449,17 @@
             pltpu.VMEM(grad.shape, F32),
             pltpu.VMEM(grad.shape, F32),
             pltpu.VMEM(grad.shape, F32),
-            pltpu.VMEM((3, 3, tile, tile), F32),
+            pltpu.VMEM((3, tile, 2 * tile), F32),
+            pltpu.VMEM((3, tile, 2 * tile), F32),
+            pltpu.VMEM((3, tile, tile), F32),
             pltpu.VMEM((3, tile, tile), F32),
             pltpu.VMEM((2, 2, 8, tile), F32),
             pltpu.VMEM((2, 2, tile, 128), F32),
             pltpu.VMEM((frame, 128), F32),
             dma((2, len(parts), stages)),
             dma((2, len(parts), stages)),
-            dma((3,)),
-            dma((3,)),
+            dma((2,)),
+            dma((2,)),
             dma((4,)),
             dma((4,)),
         ],

time: 199 us -> 182 us (0.915)
  the two profiles are of different devices: /device:TPU:28 before, /device:TPU:13 now
where the time goes in v3:
time: 182 us
  Pallas kernels  142 us (78%)
  waiting for transfers between devices  18.7 us (10%)
  local copies, waits for them, and re-layouts  11.5 us (6%)
  starting transfers between devices  7.54 us (4%)
    pallas_call x1, Pallas kernels, exchange(): pl.pallas_call(functools.partial(exchange_kernel, rows, cols, parts), out...  95.5 us
    pallas_call x1, Pallas kernels, waves(): pl.pallas_call(waves_kernel, out_shape=(jax.ShapeDtypeStruct((3, 2 * tile...  46.4 us
    ppermute x3, waiting for transfers between devices, moved(): return lax.ppermute(value, ('row', 'col'), pairs)  18.7 us
    unnamed x14, local copies, waits for them, and re-layouts  11.5 us
    ppermute x3, starting transfers between devices, moved(): return lax.ppermute(value, ('row', 'col'), pairs)  7.54 us
  transfers between devices with their start and end apart: 3, of which 2 were waited for; matrix products, arithmetic and copies ran while one was open for 0% of the time, Pallas kernels for 0%

profile of v3, /device:TPU:13, one launch (start us, length us, event | category | flops | bytes accessed | tf_op | source)
XLA Modules:
  0.0 181.8 jit_solution(15779113557281621644)
XLA Ops:
  0.6 3.6 %collective-permute-start.2 = (f32[2,256,256]{2,1,0:T(8,128)}, f32[2,256,256]{2,1,0:T(8,128)S(1)}, u32[]{:S(2)}, u32[]{:S(2)}) collective-permute-start(f32[2,256,256]{2,1,0:T(8,128)} %own.3), channel_id=1, source_target_pairs={{9,0},{10,1},{11,2},{12,3},{13,4},{14,5},{15,6},{17,8},{18,9},{19,... | collective-permute-start | bytes 1572872 | tf_op jit(solution)/shard_map/ppermute | solution.py:220
  4.2 1.7 collective-permute-start.1
  5.9 2.3 %collective-permute-start = (f32[2,256,256]{2,1,0:T(8,128)}, f32[2,256,256]{2,1,0:T(8,128)S(1)}, u32[]{:S(2)}, u32[]{:S(2)}) collective-permute-start(f32[2,256,256]{2,1,0:T(8,128)} %own.3), channel_id=1, source_target_pairs={{1,0},{2,1},{3,2},{4,3},{5,4},{6,5},{7,6},{9,8},{10,9},{11,10},{12... | collective-permute-start | bytes 1572872 | tf_op jit(solution)/shard_map/ppermute | solution.py:220
  8.9 0.1 add_multiply_fusion
  8.9 0.7 broadcast_subtract_fusion.place
  9.7 6.6 %collective-permute-done.2.diag = f32[2,256,256]{2,1,0:T(8,128)S(1)} collective-permute-done((f32[2,256,256]{2,1,0:T(8,128)}, f32[2,256,256]{2,1,0:T(8,128)S(1)}, u32[]{:S(2)}, u32[]{:S(2)}) %collective-permute-start.2) | collective-permute-done | bytes 524320 | tf_op jit(solution)/shard_map/ppermute | solution.py:220
  16.2 0.0 collective-permute-done.1.down
  16.2 12.2 %collective-permute-done.right = f32[2,256,256]{2,1,0:T(8,128)S(1)} collective-permute-done((f32[2,256,256]{2,1,0:T(8,128)}, f32[2,256,256]{2,1,0:T(8,128)S(1)}, u32[]{:S(2)}, u32[]{:S(2)}) %collective-permute-start) | collective-permute-done | bytes 524320 | tf_op jit(solution)/shard_map/ppermute | solution.py:220
  28.4 0.0 copy-start.1
  28.4 1.0 copy-done.1
  29.5 0.0 copy-start.3
  29.5 1.0 copy-done.3
  30.5 0.0 copy-start.4
  30.5 1.1 copy-done.4
  31.6 0.0 copy-start.5
  31.6 1.0 copy-done.5
  32.6 0.0 copy-start.2
  32.6 46.4 %shard_map.86 = (f32[3,512,512]{2,1,0:T(8,128)}, f32[1088,8,128]{2,1,0:T(8,128)}) custom-call(s32[2,2]{1,0:T(2,128)S(1)} %broadcast_subtract_fusion.place, s32[2]{0:T(128)S(1)} %compare_convert_fusion.live, f32[2,256,256]{2,1,0:T(8,128)S(1)} %copy-done.1, f32[2,256,256]{2,1,0:T(8,128)S(1)} %collective-permute-done.right, ...), custom_call_target="tpu_custom_call" | custom-call | flops 60000002048 | bytes 16777216 | tf_op jit(solution)/shard_map/pallas_call | solution.py:192
  79.0 0.0 copy-done.2
  79.0 0.0 copy-start
  79.0 1.9 %copy-done = f32[3,512,512]{2,1,0:T(8,128)S(1)} copy-done((f32[3,512,512]{2,1,0:T(8,128)S(1)}, f32[3,512,512]{2,1,0:T(8,128)}, u32[]{:S(2)}) %copy-start) | copy-done | bytes 3145752
  80.9 95.5 %shard_map.87 = (f32[2,256,256]{2,1,0:T(8,128)S(1)}, f32[2,8,256,256]{3,2,1,0:T(8,128)}) custom-call(f32[1088,8,128]{2,1,0:T(8,128)} %get-tuple-element.4.grad, f32[3,512,512]{2,1,0:T(8,128)S(1)} %copy-done, f32[2,256,256]{2,1,0:T(8,128)S(1)} %copy-done.2, f32[2,8,256,256]{3,2,1,0:T(8,128)} %probe.3), custom_call_target="tpu_custom_call" | custom-call | flops 4194304 | bytes 25165824 | tf_op jit(solution)/shard_map/pallas_call | solution.py:440
  176.4 0.8 copy.12
  177.2 4.6 %copy.13 = f32[2,8,256,256]{3,2,1,0:T(8,128)} copy(f32[2,8,256,256]{3,2,1,0:T(8,128)} %get-tuple-element.9) | data formatting | bytes 8388608
  (1 shorter events, 0.0 us)
Async XLA Ops:
  0.6 15.6 %collective-permute-start.2 = (f32[2,256,256]{2,1,0:T(8,128)}, f32[2,256,256]{2,1,0:T(8,128)S(1)}, u32[]{:S(2)}, u32[]{:S(2)}) collective-permute-start(f32[2,256,256]{2,1,0:T(8,128)} %own.3), channel_id=1, source_target_pairs={{9,0},{10,1},{11,2},{12,3},{13,4},{14,5},{15,6},{17,8},{18,9},{19,... | collective-permute-start | bytes 1572872 | tf_op jit(solution)/shard_map/ppermute | solution.py:220
  4.2 12.0 %collective-permute-start.1 = (f32[2,256,256]{2,1,0:T(8,128)}, f32[2,256,256]{2,1,0:T(8,128)S(1)}, u32[]{:S(2)}, u32[]{:S(2)}) collective-permute-start(f32[2,256,256]{2,1,0:T(8,128)} %own.3), channel_id=1, source_target_pairs={{8,0},{9,1},{10,2},{11,3},{12,4},{13,5},{14,6},{15,7},{16,8},{17,9... | collective-permute-start | bytes 1572872 | tf_op jit(solution)/shard_map/ppermute | solution.py:220
  5.9 22.5 %collective-permute-start = (f32[2,256,256]{2,1,0:T(8,128)}, f32[2,256,256]{2,1,0:T(8,128)S(1)}, u32[]{:S(2)}, u32[]{:S(2)}) collective-permute-start(f32[2,256,256]{2,1,0:T(8,128)} %own.3), channel_id=1, source_target_pairs={{1,0},{2,1},{3,2},{4,3},{5,4},{6,5},{7,6},{9,8},{10,9},{11,10},{12... | collective-permute-start | bytes 1572872 | tf_op jit(solution)/shard_map/ppermute | solution.py:220
  28.4 1.0 copy-start.1
  29.5 1.0 copy-start.3
  30.5 1.1 copy-start.4
  31.6 1.0 copy-start.5
  32.6 46.4 %copy-start.2 = (f32[2,256,256]{2,1,0:T(8,128)S(1)}, f32[2,256,256]{2,1,0:T(8,128)}, u32[]{:S(2)}) copy-start(f32[2,256,256]{2,1,0:T(8,128)} %own.3) | copy-start | bytes 1572868
  79.0 1.9 %copy-start = (f32[3,512,512]{2,1,0:T(8,128)S(1)}, f32[3,512,512]{2,1,0:T(8,128)}, u32[]{:S(2)}) copy-start(f32[3,512,512]{2,1,0:T(8,128)} %get-tuple-element.5.totals) | copy-start | bytes 9437188

commit v4 on v3

--- a/solution.py
+++ b/solution.py
@@ -234,6 +234,7 @@
     low = [(1, bit) for bit in range(col_bits // 2)]
     high = [(1, bit) for bit in range(col_bits // 2, col_bits)]
     orders = [core + far + low + high, core + low + high + far, core + high + far + low]
+    orders = [orders[k % 3] for k in range(len(parts))]
     stages = row_bits + col_bits
 
     def partner(axis, bit):
@@ -427,7 +428,7 @@
     modes, frame = probe.shape[1], probe.shape[2]
     used = (2 * modes + 1) * (frame // 128) * (frame // 8)
     units = -(-used // devices)
-    bounds = [units * k // 3 * devices for k in range(4)]
+    bounds = [units * k // 6 * devices for k in range(7)]
     return units * devices, [(a, b - a) for a, b in zip(bounds, bounds[1:]) if b > a]
 
 
@@ -475,7 +476,7 @@
     slots = patterns.shape[0]
     right = moved(object_field, 0, -1)
     down = moved(object_field, -1, 0)
-    diag = moved(object_field, -1, -1)
+    diag = moved(right, -1, 0)
     base = jnp.stack([lax.axis_index("row"), lax.axis_index("col")]).astype(jnp.int32) * tile
     place = offsets - base[:, None]
     live = (jnp.arange(slots, dtype=jnp.int32) < counts[0]).astype(jnp.int32)

time: 182 us -> 180 us (0.989)
  waiting for transfers between devices: 18.7 us -> 8.99 us
  Pallas kernels: 142 us -> 147 us
  starting transfers between devices: 7.54 us -> 9.37 us
    ppermute x3, waiting for transfers between devices: 18.7 us -> 8.99 us  [moved(): return lax.ppermute(value, ('row', 'col'), pairs)]
    pallas_call x1, Pallas kernels: 95.5 us -> 101 us  [exchange(): pl.pallas_call(functools.partial(exchange_kernel, rows, cols, parts), out...]
    ppermute x3, starting transfers between devices: 7.54 us -> 9.37 us  [moved(): return lax.ppermute(value, ('row', 'col'), pairs)]
  transfers between devices with their start and end apart: 3 -> 3, of which waited for: 2 -> 1; matrix products, arithmetic and copies ran while one was open for 0% -> 0% of each run, Pallas kernels for 0% -> 0%
where the time goes in v4:
time: 180 us; the launch traced here: 179 us
  Pallas kernels  147 us (82%)
  local copies, waits for them, and re-layouts  11.5 us (6%)
  starting transfers between devices  9.37 us (5%)
  waiting for transfers between devices  8.99 us (5%)
    pallas_call x1, Pallas kernels, exchange(): pl.pallas_call(functools.partial(exchange_kernel, rows, cols, parts), out...  101 us
    pallas_call x1, Pallas kernels, waves(): pl.pallas_call(waves_kernel, out_shape=(jax.ShapeDtypeStruct((3, 2 * tile...  46.4 us
    unnamed x14, local copies, waits for them, and re-layouts  11.5 us
    ppermute x3, starting transfers between devices, moved(): return lax.ppermute(value, ('row', 'col'), pairs)  9.37 us
    ppermute x3, waiting for transfers between devices, moved(): return lax.ppermute(value, ('row', 'col'), pairs)  8.99 us
  transfers between devices with their start and end apart: 3, of which 1 were waited for; matrix products, arithmetic and copies ran while one was open for 0% of the time, Pallas kernels for 0%

profile of v4, /device:TPU:13, one launch (start us, length us, event | category | flops | bytes accessed | tf_op | source)
XLA Modules:
  0.0 179.2 jit_solution(13806480562444331634)
XLA Ops:
  0.6 3.0 %collective-permute-start = (f32[2,256,256]{2,1,0:T(8,128)}, f32[2,256,256]{2,1,0:T(8,128)S(1)}, u32[]{:S(2)}, u32[]{:S(2)}) collective-permute-start(f32[2,256,256]{2,1,0:T(8,128)} %own.3), channel_id=1, source_target_pairs={{1,0},{2,1},{3,2},{4,3},{5,4},{6,5},{7,6},{9,8},{10,9},{11,10},{12... | collective-permute-start | bytes 1572872 | tf_op jit(solution)/shard_map/ppermute | solution.py:220
  3.6 2.9 %collective-permute-start.1 = (f32[2,256,256]{2,1,0:T(8,128)}, f32[2,256,256]{2,1,0:T(8,128)S(1)}, u32[]{:S(2)}, u32[]{:S(2)}) collective-permute-start(f32[2,256,256]{2,1,0:T(8,128)} %own.3), channel_id=1, source_target_pairs={{8,0},{9,1},{10,2},{11,3},{12,4},{13,5},{14,6},{15,7},{16,8},{17,9... | collective-permute-start | bytes 1572872 | tf_op jit(solution)/shard_map/ppermute | solution.py:220
  6.5 9.0 %collective-permute-done.right = f32[2,256,256]{2,1,0:T(8,128)S(1)} collective-permute-done((f32[2,256,256]{2,1,0:T(8,128)}, f32[2,256,256]{2,1,0:T(8,128)S(1)}, u32[]{:S(2)}, u32[]{:S(2)}) %collective-permute-start) | collective-permute-done | bytes 524320 | tf_op jit(solution)/shard_map/ppermute | solution.py:220
  15.5 3.5 %collective-permute-start.2 = (f32[2,256,256]{2,1,0:T(8,128)S(1)}, f32[2,256,256]{2,1,0:T(8,128)S(1)}, u32[]{:S(2)}, u32[]{:S(2)}) collective-permute-start(f32[2,256,256]{2,1,0:T(8,128)S(1)} %collective-permute-done.right), channel_id=1, source_target_pairs={{8,0},{9,1},{10,2},{11,3},{12,4},{13,5},{14,6},{15,7},{16,8},{17,9... | collective-permute-start | bytes 1572872 | tf_op jit(solution)/shard_map/ppermute | solution.py:220
  19.7 0.1 add_multiply_fusion
  19.7 0.7 broadcast_subtract_fusion.place
  20.5 0.0 collective-permute-done.1.down
  20.5 0.0 collective-permute-done.2.diag
  20.5 0.0 copy-start.1
  20.5 1.0 copy-done.1
  21.5 0.0 copy-start.3
  21.6 1.0 copy-done.3
  22.6 0.0 copy-start.4
  22.6 1.1 copy-done.4
  23.7 0.0 copy-start.5
  23.7 1.0 copy-done.5
  24.7 0.0 copy-start.2
  24.7 46.4 %shard_map.86 = (f32[3,512,512]{2,1,0:T(8,128)}, f32[1088,8,128]{2,1,0:T(8,128)}) custom-call(s32[2,2]{1,0:T(2,128)S(1)} %broadcast_subtract_fusion.place, s32[2]{0:T(128)S(1)} %compare_convert_fusion.live, f32[2,256,256]{2,1,0:T(8,128)S(1)} %copy-done.1, f32[2,256,256]{2,1,0:T(8,128)S(1)} %collective-permute-done.right, ...), custom_call_target="tpu_custom_call" | custom-call | flops 60000002048 | bytes 16777216 | tf_op jit(solution)/shard_map/pallas_call | solution.py:192
  71.1 0.0 copy-done.2
  71.1 0.0 copy-start
  71.1 1.9 %copy-done = f32[3,512,512]{2,1,0:T(8,128)S(1)} copy-done((f32[3,512,512]{2,1,0:T(8,128)S(1)}, f32[3,512,512]{2,1,0:T(8,128)}, u32[]{:S(2)}) %copy-start) | copy-done | bytes 3145752
  73.0 100.8 %shard_map.87 = (f32[2,256,256]{2,1,0:T(8,128)S(1)}, f32[2,8,256,256]{3,2,1,0:T(8,128)}) custom-call(f32[1088,8,128]{2,1,0:T(8,128)} %get-tuple-element.4.grad, f32[3,512,512]{2,1,0:T(8,128)S(1)} %copy-done, f32[2,256,256]{2,1,0:T(8,128)S(1)} %copy-done.2, f32[2,8,256,256]{3,2,1,0:T(8,128)} %probe.3), custom_call_target="tpu_custom_call" | custom-call | flops 4194304 | bytes 25165824 | tf_op jit(solution)/shard_map/pallas_call | solution.py:441
  173.8 0.8 copy.12
  174.6 4.6 %copy.13 = f32[2,8,256,256]{3,2,1,0:T(8,128)} copy(f32[2,8,256,256]{3,2,1,0:T(8,128)} %get-tuple-element.9) | data formatting | bytes 8388608
  (1 shorter events, 0.0 us)
Async XLA Ops:
  0.6 14.9 %collective-permute-start = (f32[2,256,256]{2,1,0:T(8,128)}, f32[2,256,256]{2,1,0:T(8,128)S(1)}, u32[]{:S(2)}, u32[]{:S(2)}) collective-permute-start(f32[2,256,256]{2,1,0:T(8,128)} %own.3), channel_id=1, source_target_pairs={{1,0},{2,1},{3,2},{4,3},{5,4},{6,5},{7,6},{9,8},{10,9},{11,10},{12... | collective-permute-start | bytes 1572872 | tf_op jit(solution)/shard_map/ppermute | solution.py:220
  3.6 16.9 %collective-permute-start.1 = (f32[2,256,256]{2,1,0:T(8,128)}, f32[2,256,256]{2,1,0:T(8,128)S(1)}, u32[]{:S(2)}, u32[]{:S(2)}) collective-permute-start(f32[2,256,256]{2,1,0:T(8,128)} %own.3), channel_id=1, source_target_pairs={{8,0},{9,1},{10,2},{11,3},{12,4},{13,5},{14,6},{15,7},{16,8},{17,9... | collective-permute-start | bytes 1572872 | tf_op jit(solution)/shard_map/ppermute | solution.py:220
  15.5 5.0 %collective-permute-start.2 = (f32[2,256,256]{2,1,0:T(8,128)S(1)}, f32[2,256,256]{2,1,0:T(8,128)S(1)}, u32[]{:S(2)}, u32[]{:S(2)}) collective-permute-start(f32[2,256,256]{2,1,0:T(8,128)S(1)} %collective-permute-done.right), channel_id=1, source_target_pairs={{8,0},{9,1},{10,2},{11,3},{12,4},{13,5},{14,6},{15,7},{16,8},{17,9... | collective-permute-start | bytes 1572872 | tf_op jit(solution)/shard_map/ppermute | solution.py:220
  20.5 1.0 copy-start.1
  21.5 1.0 copy-start.3
  22.6 1.1 copy-start.4
  23.7 1.0 copy-start.5
  24.7 46.4 %copy-start.2 = (f32[2,256,256]{2,1,0:T(8,128)S(1)}, f32[2,256,256]{2,1,0:T(8,128)}, u32[]{:S(2)}) copy-start(f32[2,256,256]{2,1,0:T(8,128)} %own.3) | copy-start | bytes 1572868
  71.1 1.9 %copy-start = (f32[3,512,512]{2,1,0:T(8,128)S(1)}, f32[3,512,512]{2,1,0:T(8,128)}, u32[]{:S(2)}) copy-start(f32[3,512,512]{2,1,0:T(8,128)} %get-tuple-element.5.totals) | copy-start | bytes 9437188
